TPU v7x, 128 devices: a whole 4x4x4 slice. The times are simulated.
128 devices in a mesh: req: 8 (over x, core), exp: 16 (over y, z).
Axes of the slice: x: 4, y: 4, z: 4, core: 2. Of those that a mesh axis runs over, the one named last changes fastest.
Arguments:
- latent_cache: bfloat16 [1024, 1024, 576], P(('req', 'exp')), may hold values from -6 to 6
- context_lengths: int32 [1024], P(('req', 'exp')), may hold values from 2 to 1022, as said below
- destination: int32 [1024], P(('req', 'exp')), may hold values from 0 to 1023, as said below
- query_first: bfloat16 [1024, 128, 576], P(('req', 'exp')), may hold values from -240 to 240
- latent_first: bfloat16 [1024, 576], P(('req', 'exp')), may hold values from -6 to 6
- query_second: bfloat16 [1024, 128, 576], P(('req', 'exp')), may hold values from -240 to 240
- latent_second: bfloat16 [1024, 576], P(('req', 'exp')), may hold values from -6 to 6
- hidden: bfloat16 [1024, 7168], P(('req', 'exp')), may hold values from -6 to 6
- expert_ids: int32 [1024, 4], P(('req', 'exp')), may hold values from 0 to 15, all different within a row; in each aligned block of 8 rows (0 to 7, 8 to 15, ...) at most 4 rows name the same one
- gate_weights: float32 [1024, 4], P(('req', 'exp')), may hold values from 0.1 to 1
- expert_gate: bfloat16 [16, 7168, 2048], P('exp', None, 'req'), may hold values from -0.0625 to 0.0625
- expert_up: bfloat16 [16, 7168, 2048], P('exp', None, 'req'), may hold values from -0.0625 to 0.0625
- expert_down: bfloat16 [16, 2048, 7168], P('exp', 'req'), may hold values from -0.125 to 0.125
Outputs:
- context_first: bfloat16 [1024, 128, 512], P(('req', 'exp'))
- context_second: bfloat16 [1024, 128, 512], P(('req', 'exp'))
- routed_output: bfloat16 [1024, 7168], P(('req', 'exp'))
Inputs may be any that keep to these rules, and one draw needn't show every extreme that they name: Request g sits on device g // 8 (devices in the order req, then exp) in slot g % 8. destination is a permutation that keeps every request in its exp column; on each device exactly two requests go to two different other ranks of req and exactly those two slots receive one request each from two different other ranks; all other requests keep their slot. `context_lengths`: at least 2; some request has exactly 1022. `expert_ids`: in the rows of one device no expert is named more than 4 times, and on some device some expert is named exactly 4 times.
All inputs are finite; a program needn't handle non-finite values.
Results may differ from a plain program's by a relative error of at most 0.015.
Values may be sent and summed in bfloat16 or wider, within the bound.
A program may use at most 192 MiB of HBM per device.

v0:
```python
import math

import jax
import jax.numpy as jnp
from jax import lax
from jax.sharding import PartitionSpec as P

LATENT = 512


score_scale = 1.0 / math.sqrt(192.0)


def attend(queries, key_rows, limits):
    scores = (
        jnp.einsum("rhc,rtc->rht", queries, key_rows, preferred_element_type=jnp.float32)
        * score_scale
    )
    positions = jnp.arange(key_rows.shape[1], dtype=jnp.int32)
    visible = positions[None, None, :] <= limits[:, None, None]
    scores = jnp.where(visible, scores, -jnp.inf)
    highest = jnp.max(scores, axis=2, keepdims=True)
    weights = jnp.exp(scores - highest)
    probs_bf = (weights / jnp.sum(weights, axis=2, keepdims=True)).astype(jnp.bfloat16)
    return jnp.einsum(
        "rht,rtc->rhc", probs_bf, key_rows[:, :, :LATENT], preferred_element_type=jnp.float32
    ).astype(jnp.bfloat16)


def append_rows(key_rows, new_rows, positions_at):
    positions = jnp.arange(key_rows.shape[1], dtype=jnp.int32)
    hit_mask = positions[None, :] == positions_at[:, None]
    return jnp.where(hit_mask[:, :, None], new_rows[:, None, :], key_rows)


def select_rows(chooser, values):
    return jnp.einsum(
        "ps,s...->p...", chooser.astype(jnp.bfloat16), values, preferred_element_type=jnp.float32
    ).astype(jnp.bfloat16)


def expert_apply(token_rows, gate_matrix, up_matrix, down_matrix):
    flat_rows = token_rows.reshape(-1, token_rows.shape[-1])
    gate_act = jnp.dot(flat_rows, gate_matrix, preferred_element_type=jnp.float32)
    up_act = jnp.dot(flat_rows, up_matrix, preferred_element_type=jnp.float32)
    inner_act = (jax.nn.silu(gate_act) * up_act).astype(jnp.bfloat16)
    partial_rows = jnp.dot(inner_act, down_matrix, preferred_element_type=jnp.float32).astype(
        jnp.bfloat16
    )
    return partial_rows.reshape(token_rows.shape)


def shards(
    latent_cache,
    context_lengths,
    destination,
    query_first,
    latent_first,
    query_second,
    latent_second,
    hidden,
    expert_ids,
    gate_weights,
    expert_gate,
    expert_up,
    expert_down,
):
    slot_count = latent_cache.shape[0]
    rank_count = lax.axis_size("req")
    expert_count = lax.axis_size("exp")
    my_rank = lax.axis_index("req")
    cache_first = append_rows(latent_cache, latent_first, context_lengths)
    context_first = attend(query_first, cache_first, context_lengths)
    dest_rank = destination // (expert_count * slot_count)
    dest_slot = destination % slot_count
    peer_ranks = jnp.arange(rank_count, dtype=jnp.int32)
    outgoing = (dest_rank[None, :] == peer_ranks[:, None]) & (peer_ranks[:, None] != my_rank)
    claimed = jnp.where(
        jnp.any(outgoing, axis=1),
        jnp.sum(outgoing.astype(jnp.int32) * dest_slot[None, :], axis=1),
        -1,
    )
    slot_index = jnp.arange(slot_count, dtype=jnp.int32)
    sent_lengths = jnp.sum(outgoing.astype(jnp.int32) * context_lengths[None, :], axis=1)
    arrived, arrived_lengths, arrived_slots = (
        lax.all_to_all(
            select_rows(outgoing, cache_first), "req", split_axis=0, concat_axis=0, tiled=True
        ),
        lax.all_to_all(sent_lengths, "req", split_axis=0, concat_axis=0, tiled=True),
        lax.all_to_all(claimed, "req", split_axis=0, concat_axis=0, tiled=True),
    )
    taken_mask = slot_index[:, None] == arrived_slots[None, :]
    filled = jnp.any(taken_mask, axis=1)
    cache_second = jnp.where(filled[:, None, None], select_rows(taken_mask, arrived), cache_first)
    lengths_second = jnp.where(
        filled,
        jnp.sum(taken_mask.astype(jnp.int32) * arrived_lengths[None, :], axis=1),
        context_lengths,
    ).astype(jnp.int32)
    context_second = attend(
        query_second,
        append_rows(cache_second, latent_second, lengths_second + 1),
        lengths_second + 1,
    )
    token_count = hidden.shape[0]
    choices_per = expert_ids.shape[1]
    feature_width = hidden.shape[1]
    capacity = max(2, token_count * choices_per * 2 // expert_count)
    flat_ids = expert_ids.reshape(token_count * choices_per)
    onehot = (flat_ids[:, None] == jnp.arange(expert_count, dtype=jnp.int32)[None, :]).astype(
        jnp.int32
    )
    position = jnp.sum((jnp.cumsum(onehot, axis=0) - onehot) * onehot, axis=1)
    target = flat_ids * capacity + position
    placed = (
        target[:, None] == jnp.arange(expert_count * capacity, dtype=jnp.int32)[None, :]
    ).reshape(token_count, choices_per, expert_count * capacity)
    spread = jnp.any(placed, axis=1).T.astype(jnp.bfloat16)
    outbound = (
        jnp.dot(spread, hidden, preferred_element_type=jnp.float32)
        .astype(jnp.bfloat16)
        .reshape(expert_count, capacity, feature_width)
    )
    gate_matrix = expert_gate[0]
    up_matrix = expert_up[0]
    down_matrix = expert_down[0]
    copies = jnp.broadcast_to(
        outbound[None], (rank_count, expert_count, capacity, feature_width)
    ).reshape(rank_count * expert_count, capacity, feature_width)
    partials = expert_apply(
        lax.all_to_all(copies, ("req", "exp"), split_axis=0, concat_axis=0, tiled=True),
        gate_matrix,
        up_matrix,
        down_matrix,
    )
    returned_parts = lax.all_to_all(
        partials, ("req", "exp"), split_axis=0, concat_axis=0, tiled=True
    )
    summed = jnp.sum(
        returned_parts.reshape(rank_count, expert_count, capacity, feature_width),
        axis=0,
        dtype=jnp.float32,
    )
    mixing = jnp.sum(placed.astype(jnp.float32) * gate_weights[:, :, None], axis=1)
    routed_output = jnp.dot(
        mixing,
        summed.reshape(expert_count * capacity, feature_width),
        precision=lax.Precision.HIGHEST,
        preferred_element_type=jnp.float32,
    ).astype(jnp.bfloat16)
    return (context_first, context_second, routed_output)


def solution(mesh):
    placed = (
        P(("req", "exp"), None, None),
        P(("req", "exp")),
        P(("req", "exp")),
        P(("req", "exp"), None, None),
        P(("req", "exp"), None),
        P(("req", "exp"), None, None),
        P(("req", "exp"), None),
        P(("req", "exp"), None),
        P(("req", "exp"), None),
        P(("req", "exp"), None),
        P("exp", None, "req"),
        P("exp", None, "req"),
        P("exp", "req", None),
    )
    return jax.shard_map(
        shards,
        mesh=mesh,
        in_specs=placed,
        out_specs=(
            P(("req", "exp"), None, None),
            P(("req", "exp"), None, None),
            P(("req", "exp"), None),
        ),
        check_vma=False,
    )
```

profile of v0, /device:TPU:0, one launch (start us, length us, event | category | flops | bytes accessed | tf_op | source)
XLA Modules:
  0.0 355.1 jit_solution(8821391516640091647)
XLA Ops:
  12.7 7.9 %all_to_all.30 = s32[8,1,1]{2,1,0:T(1,128)S(1)} all-to-all(s32[8,1,1]{2,1,0:T(1,128)S(1)} %copy.66), channel_id=1, replica_groups=mesh['req'=8,'exp'=16] {'req'}, dimensions={0} | all-to-all | bytes 64 | tf_op jit(solution)/shard_map/all_to_all | solution.py:89
  26.1 10.0 %all-to-all-start.3 = ((bf16[128,4,7168]{2,1,0:T(4,128)(2,1)}), bf16[128,4,7168]{2,1,0:T(4,128)(2,1)}, u32[]{:S(2)}, u32[]{:S(2)}) async-start(bf16[128,4,7168]{2,1,0:T(4,128)(2,1)} %bitcast.64), calls=%async_computation.3 | async-start | bytes 14680064 | tf_op jit(solution)/shard_map/all_to_all | solution.py:131
  36.1 14.1 %copy.62 = bf16[8,1024,576]{2,1,0:T(8,128)(2,1)} copy(bf16[8,1024,576]{1,2,0:T(8,128)(2,1)} %param.13) | data formatting | bytes 18874368 | tf_op args[0]
  50.3 10.5 %broadcast_select_fusion = bf16[8,1024,576]{2,1,0:T(8,128)(2,1)} fusion(bf16[8,1024,576]{2,1,0:T(8,128)(2,1)} %copy.62, pred[8,1024]{1,0:T(8,128)(4,1)S(1)} %get-tuple-element.10, bf16[8,576]{1,0:T(8,128)(2,1)S(1)} %copy-done.2), kind=kLoop, calls=%fused_computation.5 | loop fusion | flops 4718592 | bytes 18891776 | tf_op jit(solution)/shard_map/jit(_where)/select_n | solution.py:33
  60.8 15.4 %copy.67 = bf16[8,1024,576]{1,0,2:T(8,128)(2,1)} copy(bf16[8,1024,576]{2,1,0:T(8,128)(2,1)} %broadcast_select_fusion) | data formatting | bytes 18874368 | tf_op jit(solution)/shard_map/jit(_where)/select_n | solution.py:33
  76.2 10.0 %convolution_convert_fusion.3 = bf16[8,1024,576]{1,0,2:T(8,128)(2,1)} fusion(bf16[8,1024,576]{1,0,2:T(8,128)(2,1)} %copy.67, s32[8]{0:T(128)S(1)} %get-tuple-element.8, pred[8]{0:T(512)(128)(4,1)S(1)} %iota_compare_fusion.8), kind=kOutput, calls=%fused_computation.14 | convolution fusion | flops 80216192 | bytes 18874408 | tf_op jit(solution)/shard_map/ps,s...->p.../dot_general | solution.py:37
  86.2 12.6 %copy.68 = bf16[8,1024,576]{1,2,0:T(8,128)(2,1)} copy(bf16[8,1024,576]{1,0,2:T(8,128)(2,1)} %convolution_convert_fusion.3) | data formatting | bytes 18874368 | tf_op jit(solution)/shard_map/convert_element_type | solution.py:39
  98.8 32.2 %all-to-all-done.3 = bf16[128,4,7168]{2,1,0:T(4,128)(2,1)} async-done(((bf16[128,4,7168]{2,1,0:T(4,128)(2,1)}), bf16[128,4,7168]{2,1,0:T(4,128)(2,1)}, u32[]{:S(2)}, u32[]{:S(2)}) %all-to-all-start.3) | async-done | bytes 7340064 | tf_op jit(solution)/shard_map/all_to_all | solution.py:131
  130.9 5.6 %all-to-all-start.2 = ((bf16[8,1024,576]{1,2,0:T(8,128)(2,1)}), bf16[8,1024,576]{1,2,0:T(8,128)(2,1)}, u32[]{:S(2)}, u32[]{:S(2)}) async-start(bf16[8,1024,576]{1,2,0:T(8,128)(2,1)} %copy.68), calls=%async_computation.2 | async-start | bytes 18874368 | tf_op jit(solution)/shard_map/all_to_all | solution.py:86
  136.5 12.1 %reshape.163 = bf16[512,7168]{1,0:T(8,128)(2,1)} reshape(bf16[128,4,7168]{2,1,0:T(4,128)(2,1)} %all-to-all-done.3) | data formatting | bytes 14680064 | tf_op jit(solution)/shard_map/reshape | solution.py:43
  148.6 6.2 %fusion.15 = f32[512,256]{1,0:T(8,128)S(1)} fusion(bf16[512,7168]{1,0:T(8,128)(2,1)} %reshape.163, bf16[1,7168,256]{2,1,0:T(8,128)(2,1)} %param.23), kind=kOutput, calls=%fused_computation.30 | convolution fusion | flops 1879048192 | bytes 11534336 | tf_op jit(solution)/shard_map/dot_general | solution.py:44
  154.8 15.9 %convolution_convert_fusion = bf16[512,7168]{1,0:T(8,128)(2,1)} fusion(bf16[1,256,7168]{2,1,0:T(8,128)(2,1)} %param.25, bf16[512,7168]{1,0:T(8,128)(2,1)} %reshape.163, bf16[1,7168,256]{2,1,0:T(8,128)(2,1)} %param.24, f32[512,256]{1,0:T(8,128)S(1)} %fusion.15), kind=kOutput, calls=%fused_computation.3 | convolution fusion | flops 3762552832 | bytes 22544384 | tf_op jit(solution)/shard_map/dot_general | solution.py:47
  170.7 12.6 %reshape.164 = bf16[128,4,7168]{2,1,0:T(4,128)(2,1)} reshape(bf16[512,7168]{1,0:T(8,128)(2,1)} %convolution_convert_fusion) | data formatting | bytes 14680064 | tf_op jit(solution)/shard_map/reshape | solution.py:50
  183.4 59.0 %all-to-all-done.2 = bf16[8,1024,576]{1,2,0:T(8,128)(2,1)} async-done(((bf16[8,1024,576]{1,2,0:T(8,128)(2,1)}), bf16[8,1024,576]{1,2,0:T(8,128)(2,1)}, u32[]{:S(2)}, u32[]{:S(2)}) %all-to-all-start.2) | async-done | bytes 9437216 | tf_op jit(solution)/shard_map/all_to_all | solution.py:86
  242.4 6.0 %all-to-all-start.4 = ((bf16[128,4,7168]{2,1,0:T(4,128)(2,1)}), bf16[128,4,7168]{2,1,0:T(4,128)(2,1)}, u32[]{:S(2)}, u32[]{:S(2)}) async-start(bf16[128,4,7168]{2,1,0:T(4,128)(2,1)} %reshape.164), calls=%async_computation.4 | async-start | bytes 14680064 | tf_op jit(solution)/shard_map/all_to_all | solution.py:136
  248.5 7.5 %fusion.61 = (f32[8,128]{1,0:T(8,128)S(1)}, f32[8,128,1024]{1,2,0:T(8,128)}) fusion(pred[8,1024]{1,0:T(8,128)(4,1)S(1)} %get-tuple-element.9, bf16[8,1024,576]{2,1,0:T(8,128)(2,1)} %broadcast_select_fusion, bf16[8,128,576]{1,2,0:T(8,128)(2,1)S(1)} %copy-done), kind=kOutput, calls=%fused_computation.83 | convolution fusion | flops 1212154880 | bytes 14823424 | tf_op jit(solution)/shard_map/sub | solution.py:23
  256.0 7.0 %fusion.29 = bf16[8,128,512]{2,1,0:T(8,128)(2,1)} fusion(bf16[8,1024,576]{2,1,0:T(8,128)(2,1)} %broadcast_select_fusion, f32[8,128,1024]{1,2,0:T(8,128)} %get-tuple-element.12, f32[8,128]{1,0:T(8,128)S(1)} %get-tuple-element.11), kind=kOutput, calls=%fused_computation.40 | convolution fusion | flops 1076363264 | bytes 13635584 | tf_op jit(solution)/shard_map/rht,rtc->rhc/dot_general | solution.py:25
  263.9 12.9 %fusion.2 = bf16[8,1024,576]{1,0,2:T(8,128)(2,1)} fusion(bf16[8,1024,576]{1,2,0:T(8,128)(2,1)} %all-to-all-done.2, s32[8]{0:T(128)S(1)} %reduce), kind=kOutput, calls=%fused_computation.6 | convolution fusion | flops 75497536 | bytes 18874400 | tf_op jit(solution)/shard_map/ps,s...->p.../dot_general | solution.py:37
  276.8 15.0 %copy.70 = bf16[8,1024,576]{2,1,0:T(8,128)(2,1)} copy(bf16[8,1024,576]{1,0,2:T(8,128)(2,1)} %fusion.2) | data formatting | bytes 18874368 | tf_op jit(solution)/shard_map/ps,s...->p.../dot_general | solution.py:37
  291.8 13.4 %select_select_fusion = bf16[8,1024,576]{2,1,0:T(8,128)(2,1)} fusion(bf16[8,1024,576]{2,1,0:T(8,128)(2,1)} %copy.70, pred[8]{0:T(512)(128)(4,1)S(1)} %fusion.47, pred[8,1024]{1,0:T(8,128)(4,1)S(1)} %get-tuple-element.6, bf16[8,576]{1,0:T(8,128)(2,1)S(1)} %copy-done.3, bf16[8,1024,576]{2,1,0:T(8,128)(2,1)} %copy.62, bf16[8,576]{1,0:T(8,128)(2,1)S(1)} %copy-done.2, ...), kind=kLoop, calls=%fused_computation.4 | loop fusion | flops 14155776 | bytes 28346376 | tf_op jit(solution)/shard_map/jit(_where)/select_n | solution.py:33
  305.3 7.7 %fusion.62 = (f32[8,128]{1,0:T(8,128)S(1)}, f32[8,128,1024]{1,2,0:T(8,128)}) fusion(pred[8,1024]{1,0:T(8,128)(4,1)S(1)} %get-tuple-element.5, bf16[8,1024,576]{2,1,0:T(8,128)(2,1)} %select_select_fusion, bf16[8,128,576]{1,2,0:T(8,128)(2,1)S(1)} %copy-done.6), kind=kOutput, calls=%fused_computation.84 | convolution fusion | flops 1212154880 | bytes 14823424 | tf_op jit(solution)/shard_map/sub | solution.py:23
  313.0 7.0 %fusion.32 = bf16[8,128,512]{2,1,0:T(8,128)(2,1)} fusion(bf16[8,1024,576]{2,1,0:T(8,128)(2,1)} %select_select_fusion, f32[8,128,1024]{1,2,0:T(8,128)} %get-tuple-element.14, f32[8,128]{1,0:T(8,128)S(1)} %get-tuple-element.13), kind=kOutput, calls=%fused_computation.41 | convolution fusion | flops 1076363264 | bytes 13635584 | tf_op jit(solution)/shard_map/rht,rtc->rhc/dot_general | solution.py:25
  320.0 23.3 %all-to-all-done.4 = bf16[128,4,7168]{2,1,0:T(4,128)(2,1)} async-done(((bf16[128,4,7168]{2,1,0:T(4,128)(2,1)}), bf16[128,4,7168]{2,1,0:T(4,128)(2,1)}, u32[]{:S(2)}, u32[]{:S(2)}) %all-to-all-start.4) | async-done | bytes 7340064 | tf_op jit(solution)/shard_map/all_to_all | solution.py:136
  343.3 8.1 %convert_reduce_fusion = f32[16,4,7168]{2,1,0:T(4,128)} fusion(bf16[8,16,4,7168]{3,2,1,0:T(4,128)(2,1)} %bitcast.11), kind=kLoop, calls=%fused_computation.2 | loop fusion | flops 6881280 | bytes 9175040 | tf_op jit(solution)/shard_map/reduce_sum | solution.py:139
  (45 shorter events, 22.1 us)
Async XLA Ops:
  0.6 247.8 %copy-start = (bf16[8,128,576]{1,2,0:T(8,128)(2,1)S(1)}, bf16[8,128,576]{1,2,0:T(8,128)(2,1)}, u32[]{:S(2)}) copy-start(bf16[8,128,576]{1,2,0:T(8,128)(2,1)} %param.16) | copy-start | bytes 3538948
  3.2 9.6 %all-to-all-start = ((s32[8,1,1]{2,1,0:T(1,128)}), s32[8,1,1]{2,1,0:T(1,128)S(1)}, u32[]{:S(2)}, u32[]{:S(2)}) async-start(s32[8,1,1]{2,1,0:T(1,128)} %copy.65), calls=%async_computation | async-start | bytes 8192 | tf_op jit(solution)/shard_map/all_to_all | solution.py:90
  26.1 104.9 %all-to-all-start.3 = ((bf16[128,4,7168]{2,1,0:T(4,128)(2,1)}), bf16[128,4,7168]{2,1,0:T(4,128)(2,1)}, u32[]{:S(2)}, u32[]{:S(2)}) async-start(bf16[128,4,7168]{2,1,0:T(4,128)(2,1)} %bitcast.64), calls=%async_computation.3 | async-start | bytes 14680064 | tf_op jit(solution)/shard_map/all_to_all | solution.py:131
  36.1 14.2 %copy-start.4 = (s32[8]{0:T(128)S(1)}, s32[8]{0:T(128)}, u32[]{:S(2)}) copy-start(s32[8]{0:T(128)} %param.14) | copy-start | bytes 100
  36.1 14.2 %copy-start.2 = (bf16[8,576]{1,0:T(8,128)(2,1)S(1)}, bf16[8,576]{1,0:T(8,128)(2,1)}, u32[]{:S(2)}) copy-start(bf16[8,576]{1,0:T(8,128)(2,1)} %param.17) | copy-start | bytes 27652
  130.9 111.4 %all-to-all-start.2 = ((bf16[8,1024,576]{1,2,0:T(8,128)(2,1)}), bf16[8,1024,576]{1,2,0:T(8,128)(2,1)}, u32[]{:S(2)}, u32[]{:S(2)}) async-start(bf16[8,1024,576]{1,2,0:T(8,128)(2,1)} %copy.68), calls=%async_computation.2 | async-start | bytes 18874368 | tf_op jit(solution)/shard_map/all_to_all | solution.py:86
  183.4 65.0 %copy-start.5 = (f32[8,4]{0,1:T(4,128)S(1)}, f32[8,4]{0,1:T(4,128)}, u32[]{:S(2)}) copy-start(f32[8,4]{0,1:T(4,128)} %param.22) | copy-start | bytes 388
  242.4 100.9 %all-to-all-start.4 = ((bf16[128,4,7168]{2,1,0:T(4,128)(2,1)}), bf16[128,4,7168]{2,1,0:T(4,128)(2,1)}, u32[]{:S(2)}, u32[]{:S(2)}) async-start(bf16[128,4,7168]{2,1,0:T(4,128)(2,1)} %reshape.164), calls=%async_computation.4 | async-start | bytes 14680064 | tf_op jit(solution)/shard_map/all_to_all | solution.py:136
  276.8 15.0 %copy-start.3 = (bf16[8,576]{1,0:T(8,128)(2,1)S(1)}, bf16[8,576]{1,0:T(8,128)(2,1)}, u32[]{:S(2)}) copy-start(bf16[8,576]{1,0:T(8,128)(2,1)} %param.19) | copy-start | bytes 27652
  291.8 13.5 %copy-start.6 = (bf16[8,128,576]{1,2,0:T(8,128)(2,1)S(1)}, bf16[8,128,576]{1,2,0:T(8,128)(2,1)}, u32[]{:S(2)}) copy-start(bf16[8,128,576]{1,2,0:T(8,128)(2,1)} %param.18) | copy-start | bytes 3538948
  343.3 11.6 %copy-start.1 = (bf16[8,128,576]{1,2,0:T(8,128)(2,1)S(1)}, bf16[8,128,576]{1,2,0:T(8,128)(2,1)}, u32[]{:S(2)}) copy-start(bf16[8,128,576]{1,2,0:T(8,128)(2,1)} %param.16) | copy-start | bytes 3538948
where the time goes:
time: 361 us; the launch traced here: 355 us
  waiting for transfers between devices  116 us (32%)
  local copies, waits for them, and re-layouts  91.4 us (25%)
  matrix products  77.3 us (21%)
  other arithmetic  35.2 us (10%)
  starting transfers between devices  25.9 us (7%)
  blocking collectives  7.87 us (2%)
    all_to_all x1, waiting for transfers between devices, shards(): lax.all_to_all(select_rows(outgoing, cache_first), 'req', split_axis=0, c...  59 us
    all_to_all x1, waiting for transfers between devices, shards(): lax.all_to_all(copies, ('req', 'exp'), split_axis=0, concat_axis=0, tiled...  32.2 us
    select_n x2, other arithmetic, append_rows(): return jnp.where(hit_mask[:, :, None], new_rows[:, None, :], key_rows)  24 us
    all_to_all x1, waiting for transfers between devices, shards(): lax.all_to_all(partials, ('req', 'exp'), split_axis=0, concat_axis=0, til...  23.3 us
    dot_general x2, matrix products, select_rows(): jnp.einsum('ps,s...->p...', chooser.astype(jnp.bfloat16), values, preferr...  22.9 us
    dot_general x1, matrix products, expert_apply(): jnp.dot(inner_act, down_matrix, preferred_element_type=jnp.float32)  15.9 us
    select_n x1, local copies, waits for them, and re-layouts, append_rows(): return jnp.where(hit_mask[:, :, None], new_rows[:, None, :], key_rows)  15.4 us
    sub x2, matrix products, attend(): weights = jnp.exp(scores - highest)  15.2 us
  transfers between devices with their start and end apart: 4, of which 4 were waited for; matrix products, arithmetic and copies ran while one was open for 52% of the time, Pallas kernels for 0%

commit v1 on v0

v1 whole, which is shorter than its diff:
```python
import functools
import math

import jax
import jax.numpy as jnp
from jax import lax
from jax.experimental import pallas as pl
from jax.experimental.pallas import tpu as pltpu
from jax.sharding import PartitionSpec as P

MESH = pl.DeviceIdType.MESH
LATENT = 512
WIDTH = 576
HEADS = 128
CONTEXT = 1024
SLOTS = 8
D = 7168
HALF = D // 2
UNITS = 256
QROWS = 592
X, Y, Z = 0, 1, 2
SCALE = math.log2(math.e) / math.sqrt(192.0)
F32 = jnp.float32
BF16 = jnp.bfloat16

PARTS = (((X, Y, Z), 1280), ((X, Z, Y), 1280), ((Y, Z, X), 512), ((Z, Y, X), 512))
STARTS = (0, 1280, 2560, 3072)
NP = len(PARTS)
MIX = 128


def widths(lanes):
    tiles = lanes // 128
    first = (tiles + 1) // 2 * 128
    return ((0, first), (first, lanes - first))


def kernel(
    lengths, dest, cache, q1, q2, lat1, lat2, hidden, ids, gates, wg, wu, wd,
    out1, out2, routed,
    kt, qa, qb, c1, c2, qg, cg, gw, uw, dw, acc, latt,
    xp0, xp1, xp2, xp3,
    ra0, ra1, ra2, ra3, rb0, rb1, rb2, rb3, rc0, rc1, rc2, rc3,
    sa0, sa1, sa2, sa3, sb0, sb1, sb2, sb3, sc0, sc1, sc2, sc3,
    ag_s, ag_r, rs_s, rs_r, qs, qr, cs, cr, ws, wr, kt_sem, in_sem, o1_sem, o2_sem,
):
    xs = (xp0, xp1, xp2, xp3)
    first_in = ((ra0, ra1, ra2, ra3), (rb0, rb1, rb2, rb3), (rc0, rc1, rc2, rc3))
    last_in = ((sa0, sa1, sa2, sa3), (sb0, sb1, sb2, sb3), (sc0, sc1, sc2, sc3))
    rank = lax.axis_index("req")
    expert = lax.axis_index("exp")
    me = (rank // 2, expert // 4, expert % 4)
    core = rank % 2

    def device(axis, step):
        at = [me[0], me[1], me[2]]
        at[axis] = lax.rem(at[axis] + step, 4)
        return {"req": at[0] * 2 + core, "exp": at[1] * 4 + at[2]}

    def around(axis, step):
        return lax.rem(me[axis] + step, 4)

    sibling = {"req": me[0] * 2 + 1 - core, "exp": expert}

    fetch = [
        pltpu.make_async_copy(q1, qa, in_sem.at[0]),
        pltpu.make_async_copy(q2, qb, in_sem.at[1]),
        pltpu.make_async_copy(wg.at[0], gw.at[0], in_sem.at[2]),
        pltpu.make_async_copy(wu.at[0], uw.at[0], in_sem.at[3]),
        pltpu.make_async_copy(wd.at[0], dw.at[0], in_sem.at[4]),
    ]

    def key_copy(s):
        return pltpu.make_async_copy(cache.at[s], kt.at[s], kt_sem.at[s])

    fetch[1].start()
    fetch[0].start()
    for s in range(SLOTS):
        key_copy(s).start()

    barrier = pltpu.get_barrier_semaphore()
    partners = [sibling] + [device(a, d) for a in range(3) for d in (1, 3)]
    for partner in partners:
        pl.semaphore_signal(barrier, inc=1, device_id=partner, device_id_type=MESH)

    tokens = hidden[...].astype(F32)
    block = jnp.concatenate([tokens[:, :HALF], tokens[:, HALF:]], axis=0).astype(BF16)
    idt = ids[...]
    gatet = gates[...]
    expert_row = lax.broadcasted_iota(jnp.int32, (16, SLOTS), 0)
    mixing = jnp.zeros((16, SLOTS), F32)
    for j in range(4):
        mixing = mixing + jnp.where(expert_row == idt[j : j + 1, :], gatet[j : j + 1, :], 0.0)
    high = mixing.astype(BF16).astype(F32)
    middle = (mixing - high).astype(BF16).astype(F32)
    low = mixing - high - middle
    stacked = jnp.concatenate(
        [high, middle, low, jnp.zeros((MIX - 48, SLOTS), F32)], axis=0
    )
    stacked = jnp.concatenate([stacked, jnp.zeros((MIX, MIX - SLOTS), F32)], axis=1)
    mix_block = stacked.T[:16, :].astype(BF16)
    for p, (_, lanes) in enumerate(PARTS):
        xs[p][me[0], me[1], me[2], :, 0:lanes] = block[:, STARTS[p] : STARTS[p] + lanes]
    xs[0][me[0], me[1], me[2], :, PARTS[0][1] :] = mix_block

    pl.semaphore_wait(barrier, len(partners))

    def region(p, k, at):
        order = PARTS[p][0]
        index = [None, None, None]
        for j, axis in enumerate(order):
            index[axis] = slice(None) if j < k else (at if j == k else me[axis])
        return tuple(index)

    def spread(p, k, m):
        axis = PARTS[p][0][k]
        halves = widths(xs[p].shape[4])
        at, half, step = (
            (me[axis], 0, 1), (me[axis], 1, 3), (me[axis], 1, 1), (me[axis], 0, 3),
            (around(axis, 3), 0, 1), (around(axis, 1), 1, 3),
        )[m]
        start, size = halves[half]
        view = xs[p].at[region(p, k, at) + (slice(None), pl.ds(start, size))]
        return pltpu.make_async_remote_copy(
            src_ref=view, dst_ref=view, send_sem=ag_s.at[p, k, m], recv_sem=ag_r.at[p, k, m],
            device_id=device(axis, step), device_id_type=MESH,
        )

    def spread_start(k):
        for m in range(4):
            for p in range(NP):
                spread(p, k, m).start()

    def spread_forward(k):
        for p in range(NP):
            for m in (0, 1):
                spread(p, k, m).wait_recv()
                spread(p, k, 4 + m).start()

    def spread_wait(k, ms):
        for m in ms:
            for p in range(NP):
                spread(p, k, m).wait_recv()

    def ring(buffer, ss, rs, m):
        if m < 6:
            x, j, step = (
                (me[0], 0, 1), (me[0], 1, 3), (me[0], 1, 1), (me[0], 0, 3),
                (around(X, 3), 0, 1), (around(X, 1), 1, 3),
            )[m]
            view, target = buffer.at[x, core, j], device(X, step)
        else:
            view, target = buffer.at[around(X, (0, 3, 1, 2)[m - 6]), core], sibling
        return pltpu.make_async_remote_copy(
            src_ref=view, dst_ref=view, send_sem=ss.at[m], recv_sem=rs.at[m],
            device_id=target, device_id_type=MESH,
        )

    def ring_start(*args):
        for m in (0, 1, 2, 3, 6):
            ring(*args, m).start()

    def ring_forward(*args):
        for m in (0, 1):
            ring(*args, m).wait_recv()
            ring(*args, 4 + m).start()
        for m in (2, 3):
            ring(*args, m).wait_recv()
        for m in (7, 8):
            ring(*args, m).start()

    def ring_last(*args):
        for m in (4, 5):
            ring(*args, m).wait_recv()
        ring(*args, 9).start()

    def ring_end(*args):
        for m in (6, 7, 8, 9):
            ring(*args, m).wait_recv()
        for m in range(10):
            ring(*args, m).wait_send()

    query_ring = (qg, qs, qr)
    result_ring = (cg, cs, cr)

    spread_start(0)

    own_base = (rank * 16 + expert) * SLOTS
    slot_a = jnp.int32(SLOTS)
    slot_b = jnp.int32(-1)
    for s in range(SLOTS):
        moves = dest[s] != own_base + s
        slot_a = jnp.where(moves, jnp.minimum(slot_a, s), slot_a)
        slot_b = jnp.where(moves, s, slot_b)
    slot_a = jnp.minimum(slot_a, SLOTS - 1)
    slot_b = jnp.maximum(slot_b, 0)
    moving = (slot_a, slot_b)

    fetch[1].wait()
    lane128 = lax.broadcasted_iota(jnp.int32, (16, 128), 1)
    row16 = lax.broadcasted_iota(jnp.int32, (16, 128), 0)
    second_rows = jnp.concatenate(
        [lat2[...].astype(F32), jnp.zeros((SLOTS, 640 - WIDTH), F32)], axis=1
    )
    row8 = lax.broadcasted_iota(jnp.int32, (SLOTS, 640), 0)
    for j in range(2):
        s = moving[j]
        qg[me[0], core, j, 0:WIDTH, :] = qb[s]
        picked = jnp.sum(jnp.where(row8 == s, second_rows, 0.0), axis=0, keepdims=True)
        facts = [s, dest[s] >> 7, dest[s] & 7]
        tail = jnp.zeros((16, 128), F32)
        for i in range(5):
            tail = jnp.where(row16 == i, picked[:, i * 128 : (i + 1) * 128], tail)
        for i, fact in enumerate(facts):
            tail = jnp.where((row16 == 5) & (lane128 == i), fact.astype(F32), tail)
        qg[me[0], core, j, WIDTH:QROWS, :] = tail.astype(BF16)
    ring_start(*query_ring)

    weights = [
        pltpu.make_async_remote_copy(
            src_ref=src.at[0], dst_ref=dst.at[1], send_sem=ws.at[i], recv_sem=wr.at[i],
            device_id=sibling, device_id_type=MESH,
        )
        for i, (src, dst) in enumerate(((wg, gw), (wu, uw), (wd, dw)))
    ]
    for copy in weights:
        copy.start()
    for copy in fetch[2:]:
        copy.start()

    both = jnp.concatenate(
        [lat1[...].astype(F32), lat2[...].astype(F32)], axis=0
    )
    both = jnp.concatenate([both, jnp.zeros((16, 640 - WIDTH), F32)], axis=1)
    both = jnp.concatenate([both, jnp.zeros((112, 640), F32)], axis=0)
    latt[...] = both.T[:WIDTH, :]
    fetch[0].wait()

    lane = lax.broadcasted_iota(jnp.int32, (1, CONTEXT), 1)
    lane_col = lax.broadcasted_iota(jnp.int32, (WIDTH, 128), 1)

    def column(index):
        return jnp.sum(
            jnp.where(lane_col == index, latt[...], 0.0), axis=1, keepdims=True
        ).astype(BF16)

    def weigh(scores, limit):
        scores = jnp.where(lane <= limit, scores, -jnp.inf)
        top = jnp.max(scores, axis=1, keepdims=True)
        weight = jnp.exp2((scores - top) * SCALE)
        return weight.astype(BF16), 1.0 / jnp.sum(weight, axis=1, keepdims=True)

    def out_copy(s):
        return pltpu.make_async_copy(c1.at[s], out1.at[s], o1_sem.at[s])

    def next_phase(k):
        spread_wait(k, (2, 3, 4, 5))
        spread_start(k + 1)

    hooks = {
        1: lambda: spread_forward(0),
        2: lambda: next_phase(0),
        3: lambda: ring_forward(*query_ring),
        4: lambda: spread_forward(1),
        6: lambda: next_phase(1),
    }

    def attend(s, carry):
        for when, hook in hooks.items():
            pl.when(s == when)(hook)
        key_copy(s).wait()
        n = lengths[s]
        keys = jnp.where(
            lane == n, column(s), jnp.where(lane == n + 1, column(SLOTS + s), kt[s])
        )
        kt[s] = keys
        queries = jnp.concatenate([qa[s].T, qb[s].T], axis=0)
        scores = jnp.dot(queries, keys, preferred_element_type=F32)
        prob1, scale1 = weigh(scores[:HEADS], n)
        prob2, scale2 = weigh(scores[HEADS:], n + 1)
        result = lax.dot_general(
            jnp.concatenate([prob1, prob2], axis=0), keys[:LATENT],
            (((1,), (1,)), ((), ())), preferred_element_type=F32,
        )
        c1[s] = (result[:HEADS] * scale1).astype(BF16)
        c2[s] = (result[HEADS:] * scale2).astype(BF16)
        out_copy(s).start()
        return carry

    lax.fori_loop(0, SLOTS, attend, 0)

    ring_last(*query_ring)
    ring_end(*query_ring)

    def fact(r, j, i):
        return qg[r // 2, r % 2, j, WIDTH : WIDTH + 16, :].astype(F32)[5:6, i : i + 1]

    entries = [(r, j) for r in range(8) for j in range(2)]

    def migrant(j, carry):
        s = jnp.where(j == 0, slot_a, slot_b)
        to_rank = (dest[s] >> 7).astype(F32)
        to_slot = (dest[s] & 7).astype(F32)
        query = jnp.zeros((QROWS, HEADS), BF16)
        for r, i in entries:
            hit = (fact(r, i, 0) == to_slot) & (to_rank == r)
            query = query + qg[r // 2, r % 2, i] * jnp.where(hit, 1.0, 0.0).astype(BF16)
        tail = query[WIDTH:QROWS].astype(F32)
        tail = jnp.concatenate([tail, jnp.zeros((112, 128), F32)], axis=0).T
        col = jnp.concatenate(
            [tail[:, i : i + 1] for i in range(4)] + [tail[:64, 4:5]], axis=0
        ).astype(BF16)
        n = lengths[s]
        keys = jnp.where(lane == n + 1, col, kt[s])
        scores = jnp.dot(query[:WIDTH].T, keys, preferred_element_type=F32)
        prob, scale = weigh(scores, n + 1)
        result = lax.dot_general(
            prob, keys[:LATENT], (((1,), (1,)), ((), ())), preferred_element_type=F32
        )
        cg[me[0], core, j] = (result * scale).astype(BF16)
        return carry

    lax.fori_loop(0, 2, migrant, 0)
    ring_start(*result_ring)

    for copy in fetch[2:]:
        copy.wait()
    for copy in weights:
        copy.wait()

    def plane(p, at):
        return region(p, 2, at)

    def project(p, at, fresh):
        lanes = PARTS[p][1]
        total = None
        for h in range(2):
            rows = xs[p][plane(p, at) + (slice(h * 8, h * 8 + 8), slice(0, lanes))]
            rows = rows.astype(F32).reshape(128, lanes).astype(BF16)
            cols = slice(h * HALF + STARTS[p], h * HALF + STARTS[p] + lanes)
            part = [
                jnp.dot(rows, w[i, cols, :], preferred_element_type=F32)
                for w in (gw, uw) for i in range(2)
            ]
            total = part if total is None else [a + b for a, b in zip(total, part)]
        for i, term in enumerate(total):
            where = plane(p, at) + (slice(None), slice(i * UNITS, (i + 1) * UNITS))
            acc[where] = acc[where] + term.reshape(4, 4, 8, UNITS)

    acc[...] = jnp.zeros(acc.shape, F32)

    spread_forward(2)
    for p in range(NP):
        project(p, me[PARTS[p][0][2]], False)
    spread_wait(2, (2, 3))

    for p in range(NP):
        def near(d, carry, p=p):
            project(p, lax.rem(me[PARTS[p][0][2]] + 1 + 2 * d, 4), False)
            return carry
        lax.fori_loop(0, 2, near, 0)
    ring_forward(*result_ring)
    spread_wait(2, (4, 5))
    for p in range(NP):
        project(p, around(PARTS[p][0][2], 2), False)
    for k in range(3):
        for p in range(NP):
            for m in range(6):
                spread(p, k, m).wait_send()

    lane_mix = lax.broadcasted_iota(jnp.int32, (1, MIX), 1)
    chosen = ((lane_mix & 15) == expert) & (lane_mix < 48)

    def activate(x, carry):
        mix = xp0[x, :, :, 0:8, PARTS[0][1] :].astype(F32).reshape(128, MIX)
        weight = jnp.sum(jnp.where(chosen, mix, 0.0), axis=1, keepdims=True)
        gate = acc[x, :, :, :, 0 : 2 * UNITS].reshape(128, 2 * UNITS)
        up = acc[x, :, :, :, 2 * UNITS :].reshape(128, 2 * UNITS)
        inner = gate / (1.0 + jnp.exp(-gate)) * up * weight
        acc[x, :, :, :, 0 : 2 * UNITS] = inner.reshape(4, 4, 8, 2 * UNITS)
        return carry

    lax.fori_loop(0, 4, activate, 0)

    def expand(p, at):
        lanes = PARTS[p][1]
        inner = acc[plane(p, at) + (slice(None), slice(0, 2 * UNITS))]
        inner = inner.reshape(128, 2 * UNITS).astype(BF16)
        halves = []
        for h in range(2):
            cols = slice(h * HALF + STARTS[p], h * HALF + STARTS[p] + lanes)
            value = jnp.dot(inner[:, :UNITS], dw[0, :, cols], preferred_element_type=F32)
            value = value + jnp.dot(inner[:, UNITS:], dw[1, :, cols], preferred_element_type=F32)
            halves.append(value.reshape(4, 4, 8, lanes))
        xs[p][plane(p, at) + (slice(None), slice(0, lanes))] = jnp.concatenate(
            halves, axis=2
        ).astype(BF16)

    def back(p, k, m):
        axis, lanes = PARTS[p][0][k], PARTS[p][1]
        offset, half, step = ((2, 0, 1), (2, 1, 3), (1, 1, 1), (3, 0, 3), (1, 0, 1), (3, 1, 3))[m]
        start, size = widths(lanes)[half]
        view = xs[p].at[region(p, k, around(axis, offset)) + (slice(None), pl.ds(start, size))]
        lead = (slice(None),) * k
        if m < 2:
            first = first_in[2 - k][p]
            into = first.at[(m,) + lead + (slice(None), pl.ds(0, size))]
        else:
            into = last_in[2 - k][p].at[(m % 2,) + lead + (slice(None), pl.ds(start, size))]
        return pltpu.make_async_remote_copy(
            src_ref=view, dst_ref=into, send_sem=rs_s.at[p, k, m], recv_sem=rs_r.at[p, k, m],
            device_id=device(axis, step), device_id_type=MESH,
        )

    def back_join(p, k):
        axis, lanes = PARTS[p][0][k], PARTS[p][1]
        lead = (slice(None),) * k
        for m in (0, 1):
            back(p, k, m).wait_recv()
            start, size = widths(lanes)[m]
            where = region(p, k, around(axis, (1, 3)[m])) + (slice(None), slice(start, start + size))
            came = first_in[2 - k][p][(m,) + lead + (slice(None), slice(0, size))]
            xs[p][where] = (xs[p][where].astype(F32) + came.astype(F32)).astype(BF16)
            back(p, k, 4 + m).start()

    def back_total(p, k):
        axis, lanes = PARTS[p][0][k], PARTS[p][1]
        for m in (2, 3, 4, 5):
            back(p, k, m).wait_recv()
        where = region(p, k, me[axis]) + (slice(None), slice(0, lanes))
        came = last_in[2 - k][p]
        return (
            xs[p][where].astype(F32) + came[0].astype(F32) + came[1].astype(F32)
        ).astype(BF16), where

    for p in range(NP):
        expand(p, around(PARTS[p][0][2], 2))
        back(p, 2, 0).start()
        back(p, 2, 1).start()
    for p in range(NP):
        def near_out(d, carry, p=p):
            expand(p, lax.rem(me[PARTS[p][0][2]] + 1 + 2 * d, 4))
            return carry
        lax.fori_loop(0, 2, near_out, 0)
        back(p, 2, 2).start()
        back(p, 2, 3).start()
    for p in range(NP):
        expand(p, me[PARTS[p][0][2]])
    for p in range(NP):
        back_join(p, 2)
    ring_last(*result_ring)
    for k in (1, 0):
        for p in range(NP):
            total, where = back_total(p, k + 1)
            xs[p][where] = total
            for m in range(4):
                back(p, k, m).start()
        if k == 1:
            ring_end(*result_ring)
            for j in range(2):
                s = moving[j]
                mine = s.astype(F32)
                value = jnp.zeros((HEADS, LATENT), BF16)
                for r, i in entries:
                    hit = (fact(r, i, 1) == rank.astype(F32)) & (fact(r, i, 2) == mine)
                    value = value + cg[r // 2, r % 2, i] * jnp.where(hit, 1.0, 0.0).astype(BF16)
                for t in range(SLOTS):
                    c2[t] = jnp.where(s == t, value, c2[t])
            pltpu.make_async_copy(c2, out2, o2_sem).start()
        for p in range(NP):
            back_join(p, k)
    for p in range(NP):
        total, _ = back_total(p, 0)
        lanes = PARTS[p][1]
        for h in range(2):
            cols = slice(h * HALF + STARTS[p], h * HALF + STARTS[p] + lanes)
            routed[:, cols] = total[h * 8 : h * 8 + 8]
    for k in range(3):
        for p in range(NP):
            for m in range(6):
                back(p, k, m).wait_send()
    for s in range(SLOTS):
        out_copy(s).wait()
    pltpu.make_async_copy(c2, out2, o2_sem).wait()


def shards(
    latent_cache, context_lengths, destination, query_first, latent_first, query_second,
    latent_second, hidden, expert_ids, gate_weights, expert_gate, expert_up, expert_down,
):
    anywhere = pl.BlockSpec(memory_space=pl.ANY)
    vmem = pl.BlockSpec(memory_space=pltpu.VMEM)
    smem = pl.BlockSpec(memory_space=pltpu.SMEM)

    def lead(k):
        return (4,) * k

    xs = [
        pltpu.VMEM((4, 4, 4, 16, lanes + (MIX if p == 0 else 0)), BF16)
        for p, (_, lanes) in enumerate(PARTS)
    ]
    first_in = [
        pltpu.VMEM((2,) + lead(k) + (16, widths(lanes)[0][1]), BF16)
        for k in (2, 1, 0) for _, lanes in PARTS
    ]
    last_in = [
        pltpu.VMEM((2,) + lead(k) + (16, lanes), BF16) for k in (2, 1, 0) for _, lanes in PARTS
    ]
    dma = pltpu.SemaphoreType.DMA
    return pl.pallas_call(
        kernel,
        out_shape=(
            jax.ShapeDtypeStruct((SLOTS, HEADS, LATENT), BF16),
            jax.ShapeDtypeStruct((SLOTS, HEADS, LATENT), BF16),
            jax.ShapeDtypeStruct((SLOTS, D), BF16),
        ),
        in_specs=[smem, smem] + [anywhere] * 3 + [vmem] * 5 + [anywhere] * 3,
        out_specs=(anywhere, anywhere, vmem),
        scratch_shapes=[
            pltpu.VMEM((SLOTS, WIDTH, CONTEXT), BF16),
            pltpu.VMEM((SLOTS, WIDTH, HEADS), BF16),
            pltpu.VMEM((SLOTS, WIDTH, HEADS), BF16),
            pltpu.VMEM((SLOTS, HEADS, LATENT), BF16),
            pltpu.VMEM((SLOTS, HEADS, LATENT), BF16),
            pltpu.VMEM((4, 2, 2, QROWS, HEADS), BF16),
            pltpu.VMEM((4, 2, 2, HEADS, LATENT), BF16),
            pltpu.VMEM((2, D, UNITS), BF16),
            pltpu.VMEM((2, D, UNITS), BF16),
            pltpu.VMEM((2, UNITS, D), BF16),
            pltpu.VMEM((4, 4, 4, 8, 4 * UNITS), F32),
            pltpu.VMEM((WIDTH, 128), F32),
        ]
        + xs + first_in + last_in
        + [
            dma((NP, 3, 6)), dma((NP, 3, 6)), dma((NP, 3, 6)), dma((NP, 3, 6)),
            dma((10,)), dma((10,)), dma((10,)), dma((10,)), dma((3,)), dma((3,)),
            dma((SLOTS,)), dma((5,)), dma((SLOTS,)), dma,
        ],
        compiler_params=pltpu.CompilerParams(
            collective_id=0, has_side_effects=True, vmem_limit_bytes=64 * 1024 * 1024 - 65536
        ),
    )(
        context_lengths, destination,
        jnp.swapaxes(latent_cache, 1, 2), jnp.swapaxes(query_first, 1, 2),
        jnp.swapaxes(query_second, 1, 2), latent_first, latent_second, hidden,
        expert_ids.T, gate_weights.T, expert_gate, expert_up, expert_down,
    )


def solution(mesh):
    rows = P(("req", "exp"), None)
    cubes = P(("req", "exp"), None, None)
    flat = P(("req", "exp"))
    return jax.shard_map(
        shards,
        mesh=mesh,
        in_specs=(
            cubes, flat, flat, cubes, rows, cubes, rows, rows, rows, rows,
            P("exp", None, "req"), P("exp", None, "req"), P("exp", "req", None),
        ),
        out_specs=(cubes, cubes, rows),
        check_vma=False,
    )
```

time: 361 us -> 105 us (0.29); the launches traced: 355 us -> 105 us
  waiting for transfers between devices: 116 us -> 0 us
  Pallas kernels: 0 us -> 99.1 us
  local copies, waits for them, and re-layouts: 91.4 us -> 5.21 us
  matrix products: 77.3 us -> 0 us
  other arithmetic: 35.2 us -> 0 us
  starting transfers between devices: 25.9 us -> 0 us
  blocking collectives: 7.87 us -> 0 us
    all_to_all x4 -> x0, waiting for transfers between devices: 116 us -> none  [the longest x1 59 us: shards(): lax.all_to_all(select_rows(outgoing, cache_first), 'req', split_axis=0, c...]
    pallas_call x0 -> x1, Pallas kernels: none -> 99.1 us  [shards(): pl.pallas_call(kernel, out_shape=(jax.ShapeDtypeStruct((SLOTS, HEADS, LAT...]
    dot_general x8 -> x0, matrix products: 62.1 us -> none  [the longest x2 22.9 us: select_rows(): jnp.einsum('ps,s...->p...', chooser.astype(jnp.bfloat16), values, preferr...]
    reshape x3 -> x0, local copies, waits for them, and re-layouts: 26.7 us -> none  [the longest x1 12.6 us: expert_apply(): return partial_rows.reshape(token_rows.shape)]
    all_to_all x4 -> x0, starting transfers between devices: 25.9 us -> none  [the longest x1 9.96 us: shards(): lax.all_to_all(copies, ('req', 'exp'), split_axis=0, concat_axis=0, tiled...]
    select_n x4 -> x0, other arithmetic: 24.7 us -> none  [the longest x2 24 us: append_rows(): return jnp.where(hit_mask[:, :, None], new_rows[:, None, :], key_rows)]
    select_n x2 -> x0, local copies, waits for them, and re-layouts: 16.1 us -> none  [the longest x1 15.4 us: append_rows(): return jnp.where(hit_mask[:, :, None], new_rows[:, None, :], key_rows)]
    sub x2 -> x0, matrix products: 15.2 us -> none  [attend(): weights = jnp.exp(scores - highest)]
  transfers between devices with their start and end apart: 4 -> 0, of which waited for: 4 -> 0; matrix products, arithmetic and copies ran while one was open for 52% -> 0% of each run, Pallas kernels for 0% -> 0%
where the time goes in v1:
time: 105 us
  Pallas kernels  99.1 us (94%)
  local copies, waits for them, and re-layouts  5.21 us (5%)
    pallas_call x1, Pallas kernels, shards(): pl.pallas_call(kernel, out_shape=(jax.ShapeDtypeStruct((SLOTS, HEADS, LAT...  99.1 us
    unnamed x5, local copies, waits for them, and re-layouts  5.21 us

profile of v1, /device:TPU:0, one launch (start us, length us, event | category | flops | bytes accessed | tf_op | source)
XLA Modules:
  0.0 104.9 jit_solution(4703812660550060046)
XLA Ops:
  0.6 99.1 %shard_map.148 = (bf16[8,128,512]{2,1,0:T(8,128)(2,1)}, bf16[8,128,512]{2,1,0:T(8,128)(2,1)}, bf16[8,7168]{1,0:T(8,128)(2,1)}) custom-call(s32[8]{0:T(128)} %lengths.1, s32[8]{0:T(128)} %dest.1, bf16[8,576,1024]{2,1,0:T(8,128)(2,1)} %bitcast.5, bf16[8,576,128]{2,1,0:T(8,128)(2,1)} %bitcast.6, bf16[8,576,128]{2,1,0:T(8,128)(2,1)} %bitcast.7, ...), custom_call_target="tpu_custom_call" | custom-call | tf_op jit(solution)/shard_map/pallas_call | solution.py:510
  99.7 0.0 copy-start
  99.7 2.3 %copy.19 = bf16[8,128,512]{2,1,0:T(8,128)(2,1)} copy(bf16[8,128,512]{2,1,0:T(8,128)(2,1)} %get-tuple-element.6) | data formatting | bytes 2097152
  102.0 2.3 %copy.20 = bf16[8,128,512]{2,1,0:T(8,128)(2,1)} copy(bf16[8,128,512]{2,1,0:T(8,128)(2,1)} %get-tuple-element.7) | data formatting | bytes 2097152
  104.3 0.0 copy-done
  104.3 0.6 copy.21
Async XLA Ops:
  99.7 4.6 %copy-start = (bf16[8,7168]{1,0:T(8,128)(2,1)S(1)}, bf16[8,7168]{1,0:T(8,128)(2,1)}, u32[]{:S(2)}) copy-start(bf16[8,7168]{1,0:T(8,128)(2,1)} %get-tuple-element.8) | copy-start | bytes 344068

commit v2 on v1

v2 whole, which is shorter than its diff:
```python
import functools
import math

import jax
import jax.numpy as jnp
from jax import lax
from jax.experimental import pallas as pl
from jax.experimental.pallas import tpu as pltpu
from jax.sharding import PartitionSpec as P

MESH = pl.DeviceIdType.MESH
LATENT = 512
WIDTH = 576
HEADS = 128
CONTEXT = 1024
SLOTS = 8
D = 7168
HALF = D // 2
UNITS = 256
QROWS = 592
X, Y, Z = 0, 1, 2
SCALE = math.log2(math.e) / math.sqrt(192.0)
F32 = jnp.float32
BF16 = jnp.bfloat16

PARTS = (((X, Y, Z), 1280), ((X, Z, Y), 1280), ((Y, Z, X), 512), ((Z, Y, X), 512))
STARTS = (0, 1280, 2560, 3072)
NP = len(PARTS)
MIX_ORDER = (Y, Z, X)
EARLY = (2, 3)
LATE = (0, 1)


def widths(lanes):
    tiles = lanes // 128
    first = (tiles + 1) // 2 * 128
    return ((0, first), (first, lanes - first))


def dense_axes(p):
    order = PARTS[p][0]
    return tuple(sorted(order[:2] if p in LATE else order[:1]))


def send_phase(p):
    return 2 if p in LATE else 1


def kernel(
    lengths, dest, cache, q1, q2, lat1, lat2, hidden, ids, gates, wg, wu, wd,
    out1, out2, routed,
    kt, qa, qb, c1, c2, qg, cg, gw, uw, dw, acc, latt, xm, perm, inner, wcol,
    xb0, xb1, xb2, xb3, snd0, snd1, snd2, snd3, fin0, fin1, fin2, fin3, ret0, ret1, ret2, ret3,
    sel0, sel1, sel2, sel3, ap1, ap2, ap3,
    fb0, fb1, fb2, fb3, la0, la1, la2, la3, lb0, lb1, lb2, lb3,
    ag_s, ag_r, rs_s, rs_r, to_s, to_r, un_s, un_r, mx_s, mx_r,
    qs, qr, cs, cr, ws, wr, kt_sem, in_sem, o1_sem, o2_sem,
):
    xb = (xb0, xb1, xb2, xb3)
    snd = (snd0, snd1, snd2, snd3)
    fin = (fin0, fin1, fin2, fin3)
    ret = (ret0, ret1, ret2, ret3)
    sels = (sel0, sel1, sel2, sel3)
    partial = (acc, ap1, ap2, ap3)
    first_in = (fb0, fb1, fb2, fb3)
    last_in = (lb0, lb1, lb2, lb3)
    final_in = (la0, la1, la2, la3)
    rank = lax.axis_index("req")
    expert = lax.axis_index("exp")
    me = (rank // 2, expert // 4, expert % 4)
    core = rank % 2

    def device(axis, step):
        at = [me[0], me[1], me[2]]
        at[axis] = lax.rem(at[axis] + step, 4)
        return {"req": at[0] * 2 + core, "exp": at[1] * 4 + at[2]}

    def around(axis, step):
        return lax.rem(me[axis] + step, 4)

    sibling = {"req": me[0] * 2 + 1 - core, "exp": expert}

    fetch = [
        pltpu.make_async_copy(q1, qa, in_sem.at[0]),
        pltpu.make_async_copy(q2, qb, in_sem.at[1]),
        pltpu.make_async_copy(wg.at[0], gw.at[0], in_sem.at[2]),
        pltpu.make_async_copy(wu.at[0], uw.at[0], in_sem.at[3]),
        pltpu.make_async_copy(wd.at[0], dw.at[0], in_sem.at[4]),
    ]

    def key_copy(s):
        return pltpu.make_async_copy(cache.at[s], kt.at[s], kt_sem.at[s])

    fetch[1].start()
    fetch[0].start()
    for s in range(SLOTS):
        key_copy(s).start()

    barrier = pltpu.get_barrier_semaphore()
    partners = [sibling] + [device(a, d) for a in range(3) for d in (1, 2, 3)]
    for partner in partners:
        pl.semaphore_signal(barrier, inc=1, device_id=partner, device_id_type=MESH)

    tokens = hidden[...].astype(F32)
    block = jnp.concatenate([tokens[:, :HALF], tokens[:, HALF:]], axis=0).astype(BF16)
    idt = ids[...]
    gatet = gates[...]
    expert_row = lax.broadcasted_iota(jnp.int32, (128, SLOTS), 0)
    mixing = jnp.zeros((128, SLOTS), F32)
    for j in range(4):
        mixing = mixing + jnp.where(expert_row == idt[j : j + 1, :], gatet[j : j + 1, :], 0.0)
    mixing = jnp.concatenate([mixing, jnp.zeros((128, 128 - SLOTS), F32)], axis=1)
    xm[me[0], me[1], me[2]] = mixing.T[:SLOTS, :]
    for p, (_, lanes) in enumerate(PARTS):
        own = tuple(me[axis] for axis in dense_axes(p))
        xb[p][own] = block[:, STARTS[p] : STARTS[p] + lanes]

    pl.semaphore_wait(barrier, len(partners))

    def area(p, k, at):
        order = PARTS[p][0]
        if k == 2:
            return fin[p], (at, slice(None), slice(None))
        index = {axis: slice(None) for axis in order[:k]}
        index[order[k]] = at
        return xb[p], tuple(index.get(axis, me[axis]) for axis in dense_axes(p))

    def spread(p, k, m):
        axis = PARTS[p][0][k]
        at, half, step = (
            (me[axis], 0, 1), (me[axis], 1, 3), (me[axis], 1, 1), (me[axis], 0, 3),
            (around(axis, 3), 0, 1), (around(axis, 1), 1, 3),
        )[m]
        start, size = widths(PARTS[p][1])[half]
        buffer, index = area(p, k, at)
        view = buffer.at[index + (slice(None), pl.ds(start, size))]
        return pltpu.make_async_remote_copy(
            src_ref=view, dst_ref=view, send_sem=ag_s.at[p, k, m], recv_sem=ag_r.at[p, k, m],
            device_id=device(axis, step), device_id_type=MESH,
        )

    def first_copy(p, step):
        axis = PARTS[p][0][0]
        buffer, index = area(p, 0, me[axis])
        view = buffer.at[index]
        return pltpu.make_async_remote_copy(
            src_ref=view, dst_ref=view, send_sem=ag_s.at[p, 0, step],
            recv_sem=ag_r.at[p, 0, step], device_id=device(axis, step), device_id_type=MESH,
        )

    def spread_start(ps, k):
        for m in range(4):
            for p in ps:
                spread(p, k, m).start()

    def spread_forward(ps, k):
        for p in ps:
            for m in (0, 1):
                spread(p, k, m).wait_recv()
                spread(p, k, 4 + m).start()

    def spread_wait(ps, k, ms):
        for m in ms:
            for p in ps:
                spread(p, k, m).wait_recv()

    def mix_copy(k, step):
        index = {axis: slice(None) for axis in MIX_ORDER[:k]}
        view = xm.at[tuple(index.get(axis, me[axis]) for axis in (X, Y, Z))]
        return pltpu.make_async_remote_copy(
            src_ref=view, dst_ref=view, send_sem=mx_s.at[k, step - 1],
            recv_sem=mx_r.at[k, step - 1], device_id=device(MIX_ORDER[k], step),
            device_id_type=MESH,
        )

    def mix_start(k):
        for step in (2, 1, 3):
            mix_copy(k, step).start()

    def mix_wait(k):
        for step in (1, 2, 3):
            mix_copy(k, step).wait_recv()

    def selector(mix, row_expert, row_block):
        rows, tokens = row_expert.shape[0], mix.shape[0]
        named = lax.broadcasted_iota(jnp.int32, (rows, 128), 1) == row_expert
        weight = lax.dot_general(
            jnp.where(named, 1.0, 0.0).astype(BF16), mix.astype(BF16),
            (((1,), (1,)), ((), ())), preferred_element_type=F32,
        )
        chosen = weight > 0.0
        before = lax.broadcasted_iota(jnp.int32, (tokens, tokens), 0)
        after = lax.broadcasted_iota(jnp.int32, (tokens, tokens), 1)
        earlier = (before // 8 == after // 8) & (before < after)
        position = jnp.dot(
            jnp.where(chosen, 1.0, 0.0).astype(BF16),
            jnp.where(earlier, 1.0, 0.0).astype(BF16), preferred_element_type=F32,
        )
        slot = (lax.broadcasted_iota(jnp.int32, (rows, tokens), 0) % 4).astype(F32)
        token = lax.broadcasted_iota(jnp.int32, (rows, tokens), 1)
        hit = chosen & (position == slot) & (token // 8 == row_block)
        return jnp.where(hit, 1.0, 0.0).astype(BF16)

    def pick_slots(p):
        axis = PARTS[p][0][send_phase(p)]
        dense = dense_axes(p)
        tokens = 8 * 4 ** len(dense)
        where = tuple(slice(None) if a in dense else me[a] for a in (X, Y, Z))
        row = lax.broadcasted_iota(jnp.int32, (2 * tokens, 1), 0)
        target = row // (tokens // 2)
        row_expert = target * 4 + me[Z] if axis == Y else me[Y] * 4 + target
        row_block = (row % (tokens // 2)) // 4
        sels[p][...] = selector(xm[where].reshape(tokens, 128), row_expert, row_block)

    def compact(p, c):
        axis = PARTS[p][0][send_phase(p)]
        dense = len(dense_axes(p))
        tokens = 8 * 4 ** dense
        start, size = chunks(p)[c]
        halves = []
        for h in range(2):
            lead = (slice(None),) * dense
            tok = xb[p][lead + (slice(h * 8, h * 8 + 8), slice(start, start + size))]
            tok = tok.astype(F32).reshape(tokens, size).astype(BF16)
            got = jnp.dot(sels[p][...], tok, preferred_element_type=F32)
            halves.append(got.reshape(4, tokens // 16, 8, size))
        snd[p][:, :, :, start : start + size] = jnp.concatenate(halves, axis=2).astype(BF16)
        for step in (2, 1, 3):
            send(p, c, step).start()
        own = (me[axis],) if p in LATE else (me[X], me[axis])
        lanes = (slice(None), slice(None), slice(start, start + size))
        fin[p][own + lanes] = snd[p][(me[axis],) + lanes]

    def chunks(p):
        return widths(PARTS[p][1]) if p in LATE else ((0, PARTS[p][1]),)

    def send(p, c, step):
        axis = PARTS[p][0][send_phase(p)]
        start, size = chunks(p)[c]
        into = (me[axis],) if p in LATE else (me[X], me[axis])
        rest = (slice(None), slice(None), pl.ds(start, size))
        return pltpu.make_async_remote_copy(
            src_ref=snd[p].at[(around(axis, step),) + rest], dst_ref=fin[p].at[into + rest],
            send_sem=to_s.at[p, c, step - 1], recv_sem=to_r.at[p, c, step - 1],
            device_id=device(axis, step), device_id_type=MESH,
        )

    def send_wait(p, c):
        for step in (1, 3, 2):
            send(p, c, step).wait_recv()

    def ring(buffer, ss, rs, m):
        if m < 6:
            x, j, step = (
                (me[0], 0, 1), (me[0], 1, 3), (me[0], 1, 1), (me[0], 0, 3),
                (around(X, 3), 0, 1), (around(X, 1), 1, 3),
            )[m]
            view, target = buffer.at[x, core, j], device(X, step)
        else:
            view, target = buffer.at[around(X, (0, 3, 1, 2)[m - 6]), core], sibling
        return pltpu.make_async_remote_copy(
            src_ref=view, dst_ref=view, send_sem=ss.at[m], recv_sem=rs.at[m],
            device_id=target, device_id_type=MESH,
        )

    def ring_start(*args):
        for m in (0, 1, 2, 3, 6):
            ring(*args, m).start()

    def ring_forward(*args):
        for m in (0, 1):
            ring(*args, m).wait_recv()
            ring(*args, 4 + m).start()
        for m in (2, 3):
            ring(*args, m).wait_recv()
        for m in (7, 8):
            ring(*args, m).start()

    def ring_last(*args):
        for m in (4, 5):
            ring(*args, m).wait_recv()
        ring(*args, 9).start()

    def ring_end(*args):
        for m in (6, 7, 8, 9):
            ring(*args, m).wait_recv()
        for m in range(10):
            ring(*args, m).wait_send()

    query_ring = (qg, qs, qr)
    result_ring = (cg, cs, cr)

    mix_start(0)
    for step in (2, 1, 3):
        for p in range(NP):
            first_copy(p, step).start()

    own_base = (rank * 16 + expert) * SLOTS
    slot_a = jnp.int32(SLOTS)
    slot_b = jnp.int32(-1)
    for s in range(SLOTS):
        moves = dest[s] != own_base + s
        slot_a = jnp.where(moves, jnp.minimum(slot_a, s), slot_a)
        slot_b = jnp.where(moves, s, slot_b)
    slot_a = jnp.minimum(slot_a, SLOTS - 1)
    slot_b = jnp.maximum(slot_b, 0)
    moving = (slot_a, slot_b)

    fetch[1].wait()
    lane128 = lax.broadcasted_iota(jnp.int32, (16, 128), 1)
    row16 = lax.broadcasted_iota(jnp.int32, (16, 128), 0)
    second_rows = jnp.concatenate(
        [lat2[...].astype(F32), jnp.zeros((SLOTS, 640 - WIDTH), F32)], axis=1
    )
    row8 = lax.broadcasted_iota(jnp.int32, (SLOTS, 640), 0)
    for j in range(2):
        s = moving[j]
        qg[me[0], core, j, 0:WIDTH, :] = qb[s]
        picked = jnp.sum(jnp.where(row8 == s, second_rows, 0.0), axis=0, keepdims=True)
        facts = [s, dest[s] >> 7, dest[s] & 7]
        tail = jnp.zeros((16, 128), F32)
        for i in range(5):
            tail = jnp.where(row16 == i, picked[:, i * 128 : (i + 1) * 128], tail)
        for i, fact in enumerate(facts):
            tail = jnp.where((row16 == 5) & (lane128 == i), fact.astype(F32), tail)
        qg[me[0], core, j, WIDTH:QROWS, :] = tail.astype(BF16)
    weights = [
        pltpu.make_async_remote_copy(
            src_ref=src.at[0], dst_ref=dst.at[1], send_sem=ws.at[i], recv_sem=wr.at[i],
            device_id=sibling, device_id_type=MESH,
        )
        for i, (src, dst) in enumerate(((wg, gw), (wu, uw), (wd, dw)))
    ]
    for copy in weights:
        copy.start()
    for copy in fetch[2:]:
        copy.start()

    both = jnp.concatenate(
        [lat1[...].astype(F32), lat2[...].astype(F32)], axis=0
    )
    both = jnp.concatenate([both, jnp.zeros((16, 640 - WIDTH), F32)], axis=1)
    both = jnp.concatenate([both, jnp.zeros((112, 640), F32)], axis=0)
    latt[...] = both.T[:WIDTH, :]
    fetch[0].wait()

    lane = lax.broadcasted_iota(jnp.int32, (1, CONTEXT), 1)
    lane_col = lax.broadcasted_iota(jnp.int32, (WIDTH, 128), 1)

    def column(index):
        return jnp.sum(
            jnp.where(lane_col == index, latt[...], 0.0), axis=1, keepdims=True
        ).astype(BF16)

    def weigh(scores, limit):
        scores = jnp.where(lane <= limit, scores, -jnp.inf)
        top = jnp.max(scores, axis=1, keepdims=True)
        weight = jnp.exp2((scores - top) * SCALE)
        return weight.astype(BF16), 1.0 / jnp.sum(weight, axis=1, keepdims=True)

    def out_copy(s):
        return pltpu.make_async_copy(c1.at[s], out1.at[s], o1_sem.at[s])

    def hook1():
        for p in range(NP):
            for step in (1, 2, 3):
                first_copy(p, step).wait_recv()
        spread_start(LATE, 1)
        mix_wait(0)
        mix_start(1)
        pick_slots(2)
        compact(2, 0)

    def hook2():
        mix_wait(1)
        mix_start(2)
        pick_slots(3)
        compact(3, 0)

    def hook4():
        for p in EARLY:
            send_wait(p, 0)
        spread_start(EARLY, 2)
        ring_start(*query_ring)

    def hook6():
        mix_wait(2)
        for p in LATE:
            pick_slots(p)

    def hook7():
        spread_wait(LATE, 1, (2, 3, 4, 5))
        for c in range(2):
            for p in LATE:
                compact(p, c)

    hooks = {
        1: hook1,
        2: hook2,
        3: lambda: spread_forward(LATE, 1),
        4: hook4,
        6: hook6,
        7: hook7,
    }

    def attend(s, carry):
        for when, hook in hooks.items():
            pl.when(s == when)(hook)
        key_copy(s).wait()
        n = lengths[s]
        keys = jnp.where(
            lane == n, column(s), jnp.where(lane == n + 1, column(SLOTS + s), kt[s])
        )
        kt[s] = keys
        queries = jnp.concatenate([qa[s].T, qb[s].T], axis=0)
        scores = jnp.dot(queries, keys, preferred_element_type=F32)
        prob1, scale1 = weigh(scores[:HEADS], n)
        prob2, scale2 = weigh(scores[HEADS:], n + 1)
        result = lax.dot_general(
            jnp.concatenate([prob1, prob2], axis=0), keys[:LATENT],
            (((1,), (1,)), ((), ())), preferred_element_type=F32,
        )
        c1[s] = (result[:HEADS] * scale1).astype(BF16)
        c2[s] = (result[HEADS:] * scale2).astype(BF16)
        out_copy(s).start()
        return carry

    lax.fori_loop(0, SLOTS, attend, 0)
    spread_forward(EARLY, 2)

    everyone = xm[...].reshape(512, 128)
    lane_mix = lax.broadcasted_iota(jnp.int32, (16, 128), 1)
    weight_row = lax.dot_general(
        jnp.where(lane_mix == expert, 1.0, 0.0).astype(BF16), everyone.astype(BF16),
        (((1,), (1,)), ((), ())), preferred_element_type=F32,
    )
    chosen_rows = jnp.where(weight_row > 0.0, 1.0, 0.0)
    before = lax.broadcasted_iota(jnp.int32, (512, 512), 0)
    after = lax.broadcasted_iota(jnp.int32, (512, 512), 1)
    earlier = jnp.where((before // 8 == after // 8) & (before < after), 1.0, 0.0).astype(BF16)
    position = jnp.dot(chosen_rows.astype(BF16), earlier, preferred_element_type=F32)[0:1]
    place = jnp.where(chosen_rows[0:1] > 0.0, position, 1000.0)
    token_block = lax.broadcasted_iota(jnp.int32, (1, 512), 1) // 8
    row = lax.broadcasted_iota(jnp.int32, (256, 1), 0)
    row_slot = (row % 4).astype(F32)
    at, hi, lo = row // 64, row // 16 % 4, row // 4 % 4
    row_blocks = (
        hi * 16 + lo * 4 + at, hi * 16 + at * 4 + lo, at * 16 + lo * 4 + hi, at * 16 + hi * 4 + lo
    )

    def slots_of(p):
        hit = (token_block == row_blocks[p]) & (place == row_slot)
        return jnp.where(hit, 1.0, 0.0).astype(BF16)

    common = slots_of(0)
    for p in range(1, NP):
        perm[p - 1] = lax.dot_general(
            common, slots_of(p), (((1,), (1,)), ((), ())), preferred_element_type=F32
        ).astype(BF16)
    rest = jnp.where(lane_mix[0:1] == expert, everyone, 0.0)
    weights_here = jnp.zeros((256, 128), F32)
    for _ in range(3):
        term = rest.astype(BF16)
        weights_here = weights_here + jnp.dot(common, term, preferred_element_type=F32)
        rest = rest - term.astype(F32)
    wcol[...] = jnp.broadcast_to(jnp.sum(weights_here, axis=1, keepdims=True), (256, 128))

    ring_forward(*query_ring)

    for copy in fetch[2:]:
        copy.wait()
    for copy in weights:
        copy.wait()

    def project(p, c):
        start, size = chunks(p)[c]
        lead = (slice(None),) * (len(fin[p].shape) - 2)
        for h in range(2):
            rows = fin[p][lead + (slice(h * 8, h * 8 + 8), slice(start, start + size))]
            rows = rows.astype(F32).reshape(256, size).astype(BF16)
            begin = h * HALF + STARTS[p] + start
            for i in range(4):
                w = (gw, uw)[i // 2]
                term = jnp.dot(rows, w[i % 2, begin : begin + size, :], preferred_element_type=F32)
                cols = slice(i * UNITS, (i + 1) * UNITS)
                if p > 0 and c == 0 and h == 0:
                    partial[p][:, cols] = term
                else:
                    partial[p][:, cols] = partial[p][:, cols] + term

    def merge(p):
        for i in range(4):
            cols = slice(i * UNITS, (i + 1) * UNITS)
            value = partial[p][:, cols]
            high = value.astype(BF16)
            low = (value - high.astype(F32)).astype(BF16)
            moved = jnp.dot(perm[p - 1], high, preferred_element_type=F32)
            moved = moved + jnp.dot(perm[p - 1], low, preferred_element_type=F32)
            acc[:, cols] = acc[:, cols] + moved

    acc[...] = jnp.zeros(acc.shape, F32)

    for p in LATE:
        send_wait(p, 0)
        project(p, 0)
    spread_wait(EARLY, 2, (2, 3, 4, 5))
    for p in EARLY:
        project(p, 0)
        merge(p)
    ring_last(*query_ring)
    for p in (1, 0):
        send_wait(p, 1)
        project(p, 1)
    merge(1)
    for p in range(NP):
        for m in range(6):
            spread(p, 1 if p in LATE else 2, m).wait_send()
        for step in (1, 2, 3):
            first_copy(p, step).wait_send()
        for c in range(len(chunks(p))):
            for step in (1, 2, 3):
                send(p, c, step).wait_send()
    for k in range(3):
        for step in (1, 2, 3):
            mix_copy(k, step).wait_send()

    for i in range(2):
        cols = slice(i * UNITS, (i + 1) * UNITS)
        gate = acc[:, cols]
        up = acc[:, 2 * UNITS + i * UNITS : 2 * UNITS + (i + 1) * UNITS]
        inner[0, :, cols] = (gate / (1.0 + jnp.exp(-gate)) * up * wcol[:, 0:1]).astype(BF16)
    for p in range(1, NP):
        inner[p] = lax.dot_general(
            perm[p - 1], inner[0], (((0,), (0,)), ((), ())), preferred_element_type=F32
        ).astype(BF16)

    def expand(p, c):
        start, size = chunks(p)[c]
        halves = []
        for h in range(2):
            begin = h * HALF + STARTS[p] + start
            cols = slice(begin, begin + size)
            value = jnp.dot(inner[p, :, :UNITS], dw[0, :, cols], preferred_element_type=F32)
            value = value + jnp.dot(
                inner[p, :, UNITS:], dw[1, :, cols], preferred_element_type=F32
            )
            halves.append(value.reshape(fin[p].shape[:-2] + (8, size)))
        lead = (slice(None),) * (len(fin[p].shape) - 1)
        fin[p][lead + (slice(start, start + size),)] = jnp.concatenate(
            halves, axis=len(fin[p].shape) - 2
        ).astype(BF16)

    def unsend(p, c, step):
        axis = PARTS[p][0][send_phase(p)]
        start, size = chunks(p)[c]
        other = around(axis, step)
        rest = (slice(None), slice(None), pl.ds(start, size))
        return pltpu.make_async_remote_copy(
            src_ref=fin[p].at[((other,) if p in LATE else (me[X], other)) + rest],
            dst_ref=ret[p].at[(me[axis],) + rest],
            send_sem=un_s.at[p, c, step - 1], recv_sem=un_r.at[p, c, step - 1],
            device_id=device(axis, step), device_id_type=MESH,
        )

    def unsend_own(p):
        axis = PARTS[p][0][send_phase(p)]
        ret[p][me[axis]] = fin[p][(me[axis],) if p in LATE else (me[X], me[axis])]

    def restore(p, c):
        start, size = chunks(p)[c]
        dense = len(dense_axes(p))
        tokens = 8 * 4 ** dense
        for step in (1, 3, 2):
            unsend(p, c, step).wait_recv()
        halves = []
        for h in range(2):
            rows = ret[p][:, :, h * 8 : h * 8 + 8, start : start + size].astype(F32)
            rows = rows.reshape(2 * tokens, size).astype(BF16)
            value = lax.dot_general(
                sels[p][...], rows, (((0,), (0,)), ((), ())), preferred_element_type=F32
            )
            halves.append(value.reshape((4,) * dense + (8, size)))
        lead = (slice(None),) * (dense + 1)
        xb[p][lead + (slice(start, start + size),)] = jnp.concatenate(
            halves, axis=dense
        ).astype(BF16)

    def back(p, k, m):
        axis, lanes = PARTS[p][0][k], PARTS[p][1]
        offset, half, step = ((2, 0, 1), (2, 1, 3), (1, 1, 1), (3, 0, 3), (1, 0, 1), (3, 1, 3))[m]
        start, size = widths(lanes)[half]
        buffer, index = area(p, k, around(axis, offset))
        view = buffer.at[index + (slice(None), pl.ds(start, size))]
        lead = (slice(None),) * k
        if m < 2:
            into = first_in[p].at[(m,) + lead + (slice(None), pl.ds(0, size))]
        else:
            into = last_in[p].at[(m % 2,) + lead + (slice(None), pl.ds(start, size))]
        return pltpu.make_async_remote_copy(
            src_ref=view, dst_ref=into, send_sem=rs_s.at[p, k, m], recv_sem=rs_r.at[p, k, m],
            device_id=device(axis, step), device_id_type=MESH,
        )

    def back_join(p, k):
        axis, lanes = PARTS[p][0][k], PARTS[p][1]
        lead = (slice(None),) * k
        for m in (0, 1):
            back(p, k, m).wait_recv()
            start, size = widths(lanes)[m]
            buffer, index = area(p, k, around(axis, (1, 3)[m]))
            where = index + (slice(None), slice(start, start + size))
            came = first_in[p][(m,) + lead + (slice(None), slice(0, size))]
            buffer[where] = (buffer[where].astype(F32) + came.astype(F32)).astype(BF16)
            back(p, k, 4 + m).start()

    def back_total(p, k):
        axis = PARTS[p][0][k]
        for m in (2, 3, 4, 5):
            back(p, k, m).wait_recv()
        buffer, index = area(p, k, me[axis])
        came = last_in[p]
        total = buffer[index].astype(F32) + came[0].astype(F32) + came[1].astype(F32)
        return total.astype(BF16), buffer, index

    def back_start(p, k):
        for m in range(4):
            back(p, k, m).start()

    def last_copy(p, step):
        axis = PARTS[p][0][0]
        buffer, index = area(p, 0, around(axis, step))
        return pltpu.make_async_remote_copy(
            src_ref=buffer.at[index], dst_ref=final_in[p].at[step - 1],
            send_sem=rs_s.at[p, 0, step], recv_sem=rs_r.at[p, 0, step],
            device_id=device(axis, step), device_id_type=MESH,
        )

    def last_start(p):
        for step in (2, 1, 3):
            last_copy(p, step).start()

    def last_total(p):
        buffer, index = area(p, 0, me[PARTS[p][0][0]])
        total = buffer[index].astype(F32)
        for step in (1, 3, 2):
            last_copy(p, step).wait_recv()
            total = total + final_in[p][step - 1].astype(F32)
        return total.astype(BF16)

    def expand_late(c):
        for p in LATE:
            expand(p, c)
            for step in (2, 1, 3):
                unsend(p, c, step).start()

    expand_late(0)
    for p in EARLY:
        expand(p, 0)
        back_start(p, 2)
    expand_late(1)
    for p in LATE:
        unsend_own(p)
    ring_end(*query_ring)

    def fact(r, j, i):
        return qg[r // 2, r % 2, j, WIDTH : WIDTH + 16, :].astype(F32)[5:6, i : i + 1]

    entries = [(r, j) for r in range(8) for j in range(2)]

    def migrant(j, carry):
        s = jnp.where(j == 0, slot_a, slot_b)
        to_rank = (dest[s] >> 7).astype(F32)
        to_slot = (dest[s] & 7).astype(F32)
        query = jnp.zeros((QROWS, HEADS), BF16)
        for r, i in entries:
            hit = (fact(r, i, 0) == to_slot) & (to_rank == r)
            query = query + qg[r // 2, r % 2, i] * jnp.where(hit, 1.0, 0.0).astype(BF16)
        tail = query[WIDTH:QROWS].astype(F32)
        tail = jnp.concatenate([tail, jnp.zeros((112, 128), F32)], axis=0).T
        col = jnp.concatenate(
            [tail[:, i : i + 1] for i in range(4)] + [tail[:64, 4:5]], axis=0
        ).astype(BF16)
        n = lengths[s]
        keys = jnp.where(lane == n + 1, col, kt[s])
        scores = jnp.dot(query[:WIDTH].T, keys, preferred_element_type=F32)
        prob, scale = weigh(scores, n + 1)
        result = lax.dot_general(
            prob, keys[:LATENT], (((1,), (1,)), ((), ())), preferred_element_type=F32
        )
        cg[me[0], core, j] = (result * scale).astype(BF16)
        return carry

    lax.fori_loop(0, 2, migrant, 0)
    ring_start(*result_ring)

    for p in EARLY:
        back_join(p, 2)
    for p in LATE:
        restore(p, 0)
        back(p, 1, 0).start()
        back(p, 1, 3).start()
    ring_forward(*result_ring)
    for p in EARLY:
        total, buffer, index = back_total(p, 2)
        buffer[index] = total
        for step in (2, 1, 3):
            unsend(p, 0, step).start()
        unsend_own(p)
    for p in LATE:
        restore(p, 1)
        back(p, 1, 1).start()
        back(p, 1, 2).start()
    ring_last(*result_ring)
    for p in LATE:
        back_join(p, 1)
    for p in EARLY:
        restore(p, 0)
        last_start(p)
    for p in LATE:
        total, buffer, index = back_total(p, 1)
        buffer[index] = total
        last_start(p)
    ring_end(*result_ring)
    for j in range(2):
        s = moving[j]
        mine = s.astype(F32)
        value = jnp.zeros((HEADS, LATENT), BF16)
        for r, i in entries:
            hit = (fact(r, i, 1) == rank.astype(F32)) & (fact(r, i, 2) == mine)
            value = value + cg[r // 2, r % 2, i] * jnp.where(hit, 1.0, 0.0).astype(BF16)
        for t in range(SLOTS):
            c2[t] = jnp.where(s == t, value, c2[t])
    pltpu.make_async_copy(c2, out2, o2_sem).start()
    for p in EARLY + LATE:
        total = last_total(p)
        lanes = PARTS[p][1]
        for h in range(2):
            cols = slice(h * HALF + STARTS[p], h * HALF + STARTS[p] + lanes)
            routed[:, cols] = total[h * 8 : h * 8 + 8]
    for p in range(NP):
        for m in range(6):
            back(p, 1 if p in LATE else 2, m).wait_send()
        for step in (1, 2, 3):
            last_copy(p, step).wait_send()
        for c in range(len(chunks(p))):
            for step in (1, 2, 3):
                unsend(p, c, step).wait_send()
    for s in range(SLOTS):
        out_copy(s).wait()
    pltpu.make_async_copy(c2, out2, o2_sem).wait()


def finish(first, second, tokens, out1, out2, routed, held, sem_in, sem_out):
    pairs = [(i, s) for i in range(2) for s in range(0, SLOTS, 2)]
    sources, targets = (first, second), (out1, out2)

    def inward(i, s):
        return pltpu.make_async_copy(
            sources[i].at[pl.ds(s, 2)], held.at[i, pl.ds(s, 2)], sem_in.at[i, s]
        )

    def outward(i, s):
        return pltpu.make_async_copy(
            held.at[i, pl.ds(s, 2)], targets[i].at[pl.ds(s, 2)], sem_out.at[i, s]
        )

    for pair in pairs:
        inward(*pair).start()
    routed[...] = tokens[...]
    for pair in pairs:
        inward(*pair).wait()
        outward(*pair).start()
    for pair in pairs:
        outward(*pair).wait()


def shards(
    latent_cache, context_lengths, destination, query_first, latent_first, query_second,
    latent_second, hidden, expert_ids, gate_weights, expert_gate, expert_up, expert_down,
):
    anywhere = pl.BlockSpec(memory_space=pl.ANY)
    vmem = pl.BlockSpec(memory_space=pltpu.VMEM)
    smem = pl.BlockSpec(memory_space=pltpu.SMEM)

    def each(shape):
        return [pltpu.VMEM(shape(p, PARTS[p][1]), BF16) for p in range(NP)]

    def groups(p):
        return 8 if p in LATE else 2

    def ring_lead(p):
        return (4,) if p in LATE else (4, 2)

    buffers = (
        each(lambda p, lanes: (4,) * len(dense_axes(p)) + (16, lanes))
        + each(lambda p, lanes: (4, groups(p), 16, lanes))
        + each(lambda p, lanes: (4, 8, 16, lanes) if p in LATE else (4, 4, 2, 16, lanes))
        + each(lambda p, lanes: (4, groups(p), 16, lanes))
        + each(lambda p, lanes: (32 * groups(p), 16 * groups(p)))
        + [pltpu.VMEM((256, 4 * UNITS), F32) for _ in range(NP - 1)]
        + each(lambda p, lanes: (2,) + ring_lead(p) + (16, widths(lanes)[0][1]))
        + each(lambda p, lanes: (3, 16, lanes))
        + each(lambda p, lanes: (2,) + ring_lead(p) + (16, lanes))
    )
    dma = pltpu.SemaphoreType.DMA
    shapes = (
        jax.ShapeDtypeStruct((SLOTS, HEADS, LATENT), BF16),
        jax.ShapeDtypeStruct((SLOTS, HEADS, LATENT), BF16),
        jax.ShapeDtypeStruct((SLOTS, D), BF16),
    )
    results = pl.pallas_call(
        kernel,
        out_shape=shapes,
        in_specs=[smem, smem] + [anywhere] * 3 + [vmem] * 5 + [anywhere] * 3,
        out_specs=(anywhere, anywhere, vmem),
        scratch_shapes=[
            pltpu.VMEM((SLOTS, WIDTH, CONTEXT), BF16),
            pltpu.VMEM((SLOTS, WIDTH, HEADS), BF16),
            pltpu.VMEM((SLOTS, WIDTH, HEADS), BF16),
            pltpu.VMEM((SLOTS, HEADS, LATENT), BF16),
            pltpu.VMEM((SLOTS, HEADS, LATENT), BF16),
            pltpu.VMEM((4, 2, 2, QROWS, HEADS), BF16),
            pltpu.VMEM((4, 2, 2, HEADS, LATENT), BF16),
            pltpu.VMEM((2, D, UNITS), BF16),
            pltpu.VMEM((2, D, UNITS), BF16),
            pltpu.VMEM((2, UNITS, D), BF16),
            pltpu.VMEM((256, 4 * UNITS), F32),
            pltpu.VMEM((WIDTH, 128), F32),
            pltpu.VMEM((4, 4, 4, SLOTS, 128), F32),
            pltpu.VMEM((3, 256, 256), BF16),
            pltpu.VMEM((NP, 256, 2 * UNITS), BF16),
            pltpu.VMEM((256, 128), F32),
        ]
        + buffers
        + [
            dma((NP, 3, 6)), dma((NP, 3, 6)), dma((NP, 3, 6)), dma((NP, 3, 6)),
            dma((NP, 2, 3)), dma((NP, 2, 3)), dma((NP, 2, 3)), dma((NP, 2, 3)),
            dma((3, 3)), dma((3, 3)),
            dma((10,)), dma((10,)), dma((10,)), dma((10,)), dma((3,)), dma((3,)),
            dma((SLOTS,)), dma((5,)), dma((SLOTS,)), dma,
        ],
        compiler_params=pltpu.CompilerParams(
            collective_id=0, has_side_effects=True, vmem_limit_bytes=64 * 1024 * 1024 - 65536
        ),
    )(
        context_lengths, destination,
        jnp.swapaxes(latent_cache, 1, 2), jnp.swapaxes(query_first, 1, 2),
        jnp.swapaxes(query_second, 1, 2), latent_first, latent_second, hidden,
        expert_ids.T, gate_weights.T, expert_gate, expert_up, expert_down,
    )
    return pl.pallas_call(
        finish,
        out_shape=shapes,
        in_specs=[anywhere, anywhere, vmem],
        out_specs=(anywhere, anywhere, vmem),
        scratch_shapes=[
            pltpu.VMEM((2, SLOTS, HEADS, LATENT), BF16), dma((2, SLOTS)), dma((2, SLOTS)),
        ],
    )(*results)


def solution(mesh):
    rows = P(("req", "exp"), None)
    cubes = P(("req", "exp"), None, None)
    flat = P(("req", "exp"))
    return jax.shard_map(
        shards,
        mesh=mesh,
        in_specs=(
            cubes, flat, flat, cubes, rows, cubes, rows, rows, rows, rows,
            P("exp", None, "req"), P("exp", None, "req"), P("exp", "req", None),
        ),
        out_specs=(cubes, cubes, rows),
        check_vma=False,
    )
```

time: 105 us -> 87.5 us (0.83)
  Pallas kernels: 99.1 us -> 86 us
  local copies, waits for them, and re-layouts: 5.21 us -> 0 us
    pallas_call x1 -> x2, Pallas kernels: 99.1 us -> 86 us  [the longest x1 81.9 us: shards(): pl.pallas_call(kernel, out_shape=shapes, in_specs=[smem, smem] + [anywher...]
    unnamed x5 -> x0, local copies, waits for them, and re-layouts: 5.21 us -> none
where the time goes in v2:
time: 87.5 us; the launch traced here: 86.8 us
  Pallas kernels  86 us (98%)
    pallas_call x1, Pallas kernels, shards(): pl.pallas_call(kernel, out_shape=shapes, in_specs=[smem, smem] + [anywher...  81.9 us
    pallas_call x1, Pallas kernels, shards(): pl.pallas_call(finish, out_shape=shapes, in_specs=[anywhere, anywhere, vm...  4.08 us

profile of v2, /device:TPU:0, one launch (start us, length us, event | category | flops | bytes accessed | tf_op | source)
XLA Modules:
  0.0 86.8 jit_solution(12825948480049759562)
XLA Ops:
  0.6 81.9 %shard_map.148 = (bf16[8,128,512]{2,1,0:T(8,128)(2,1)}, bf16[8,128,512]{2,1,0:T(8,128)(2,1)}, bf16[8,7168]{1,0:T(8,128)(2,1)}) custom-call(s32[8]{0:T(128)} %lengths.1, s32[8]{0:T(128)} %dest.1, bf16[8,576,1024]{2,1,0:T(8,128)(2,1)} %bitcast.5, bf16[8,576,128]{2,1,0:T(8,128)(2,1)} %bitcast.6, bf16[8,576,128]{2,1,0:T(8,128)(2,1)} %bitcast.7, ...), custom_call_target="tpu_custom_call" | custom-call | tf_op jit(solution)/shard_map/pallas_call | solution.py:811
  82.5 4.1 %shard_map.149 = (bf16[8,128,512]{2,1,0:T(8,128)(2,1)}, bf16[8,128,512]{2,1,0:T(8,128)(2,1)}, bf16[8,7168]{1,0:T(8,128)(2,1)}) custom-call(bf16[8,128,512]{2,1,0:T(8,128)(2,1)} %get-tuple-element.6.first, bf16[8,128,512]{2,1,0:T(8,128)(2,1)} %get-tuple-element.7.second, bf16[8,7168]{1,0:T(8,128)(2,1)} %get-tuple-element.8.tokens), custom_call_target="tpu_custom_call" | custom-call | tf_op jit(solution)/shard_map/pallas_call | solution.py:851

commit v3 on v2

--- a/solution.py
+++ b/solution.py
@@ -23,8 +23,8 @@
 F32 = jnp.float32
 BF16 = jnp.bfloat16
 
-PARTS = (((X, Y, Z), 1280), ((X, Z, Y), 1280), ((Y, Z, X), 512), ((Z, Y, X), 512))
-STARTS = (0, 1280, 2560, 3072)
+PARTS = (((X, Y, Z), 1408), ((X, Z, Y), 1408), ((Y, Z, X), 384), ((Z, Y, X), 384))
+STARTS = (0, 1408, 2816, 3200)
 NP = len(PARTS)
 MIX_ORDER = (Y, Z, X)
 EARLY = (2, 3)
@@ -51,7 +51,7 @@
     out1, out2, routed,
     kt, qa, qb, c1, c2, qg, cg, gw, uw, dw, acc, latt, xm, perm, inner, wcol,
     xb0, xb1, xb2, xb3, snd0, snd1, snd2, snd3, fin0, fin1, fin2, fin3, ret0, ret1, ret2, ret3,
-    sel0, sel1, sel2, sel3, ap1, ap2, ap3,
+    sel0, sel1, sel2, sel3,
     fb0, fb1, fb2, fb3, la0, la1, la2, la3, lb0, lb1, lb2, lb3,
     ag_s, ag_r, rs_s, rs_r, to_s, to_r, un_s, un_r, mx_s, mx_r,
     qs, qr, cs, cr, ws, wr, kt_sem, in_sem, o1_sem, o2_sem,
@@ -61,7 +61,6 @@
     fin = (fin0, fin1, fin2, fin3)
     ret = (ret0, ret1, ret2, ret3)
     sels = (sel0, sel1, sel2, sel3)
-    partial = (acc, ap1, ap2, ap3)
     first_in = (fb0, fb1, fb2, fb3)
     last_in = (lb0, lb1, lb2, lb3)
     final_in = (la0, la1, la2, la3)
@@ -137,15 +136,6 @@
         return pltpu.make_async_remote_copy(
             src_ref=view, dst_ref=view, send_sem=ag_s.at[p, k, m], recv_sem=ag_r.at[p, k, m],
             device_id=device(axis, step), device_id_type=MESH,
-        )
-
-    def first_copy(p, step):
-        axis = PARTS[p][0][0]
-        buffer, index = area(p, 0, me[axis])
-        view = buffer.at[index]
-        return pltpu.make_async_remote_copy(
-            src_ref=view, dst_ref=view, send_sem=ag_s.at[p, 0, step],
-            recv_sem=ag_r.at[p, 0, step], device_id=device(axis, step), device_id_type=MESH,
         )
 
     def spread_start(ps, k):
@@ -291,9 +281,19 @@
     result_ring = (cg, cs, cr)
 
     mix_start(0)
-    for step in (2, 1, 3):
-        for p in range(NP):
-            first_copy(p, step).start()
+    spread_start(range(NP), 0)
+
+    weights = [
+        pltpu.make_async_remote_copy(
+            src_ref=src.at[0], dst_ref=dst.at[1], send_sem=ws.at[i], recv_sem=wr.at[i],
+            device_id=sibling, device_id_type=MESH,
+        )
+        for i, (src, dst) in enumerate(((wg, gw), (wu, uw), (wd, dw)))
+    ]
+    for copy in weights:
+        copy.start()
+    for copy in fetch[2:]:
+        copy.start()
 
     own_base = (rank * 16 + expert) * SLOTS
     slot_a = jnp.int32(SLOTS)
@@ -324,18 +324,6 @@
         for i, fact in enumerate(facts):
             tail = jnp.where((row16 == 5) & (lane128 == i), fact.astype(F32), tail)
         qg[me[0], core, j, WIDTH:QROWS, :] = tail.astype(BF16)
-    weights = [
-        pltpu.make_async_remote_copy(
-            src_ref=src.at[0], dst_ref=dst.at[1], send_sem=ws.at[i], recv_sem=wr.at[i],
-            device_id=sibling, device_id_type=MESH,
-        )
-        for i, (src, dst) in enumerate(((wg, gw), (wu, uw), (wd, dw)))
-    ]
-    for copy in weights:
-        copy.start()
-    for copy in fetch[2:]:
-        copy.start()
-
     both = jnp.concatenate(
         [lat1[...].astype(F32), lat2[...].astype(F32)], axis=0
     )
@@ -362,9 +350,8 @@
         return pltpu.make_async_copy(c1.at[s], out1.at[s], o1_sem.at[s])
 
     def hook1():
-        for p in range(NP):
-            for step in (1, 2, 3):
-                first_copy(p, step).wait_recv()
+        spread_forward(range(NP), 0)
+        spread_wait(range(NP), 0, (2, 3, 4, 5))
         spread_start(LATE, 1)
         mix_wait(0)
         mix_start(1)
@@ -389,6 +376,7 @@
             pick_slots(p)
 
     def hook7():
+        hook6()
         spread_wait(LATE, 1, (2, 3, 4, 5))
         for c in range(2):
             for p in LATE:
@@ -399,8 +387,7 @@
         2: hook2,
         3: lambda: spread_forward(LATE, 1),
         4: hook4,
-        6: hook6,
-        7: hook7,
+        5: hook7,
     }
 
     def attend(s, carry):
@@ -467,9 +454,7 @@
 
     ring_forward(*query_ring)
 
-    for copy in fetch[2:]:
-        copy.wait()
-    for copy in weights:
+    for copy in fetch[2:4] + weights[:2]:
         copy.wait()
 
     def project(p, c):
@@ -478,25 +463,14 @@
         for h in range(2):
             rows = fin[p][lead + (slice(h * 8, h * 8 + 8), slice(start, start + size))]
             rows = rows.astype(F32).reshape(256, size).astype(BF16)
+            if p > 0:
+                rows = jnp.dot(perm[p - 1], rows, preferred_element_type=F32).astype(BF16)
             begin = h * HALF + STARTS[p] + start
             for i in range(4):
                 w = (gw, uw)[i // 2]
                 term = jnp.dot(rows, w[i % 2, begin : begin + size, :], preferred_element_type=F32)
                 cols = slice(i * UNITS, (i + 1) * UNITS)
-                if p > 0 and c == 0 and h == 0:
-                    partial[p][:, cols] = term
-                else:
-                    partial[p][:, cols] = partial[p][:, cols] + term
-
-    def merge(p):
-        for i in range(4):
-            cols = slice(i * UNITS, (i + 1) * UNITS)
-            value = partial[p][:, cols]
-            high = value.astype(BF16)
-            low = (value - high.astype(F32)).astype(BF16)
-            moved = jnp.dot(perm[p - 1], high, preferred_element_type=F32)
-            moved = moved + jnp.dot(perm[p - 1], low, preferred_element_type=F32)
-            acc[:, cols] = acc[:, cols] + moved
+                acc[:, cols] = acc[:, cols] + term
 
     acc[...] = jnp.zeros(acc.shape, F32)
 
@@ -506,17 +480,13 @@
     spread_wait(EARLY, 2, (2, 3, 4, 5))
     for p in EARLY:
         project(p, 0)
-        merge(p)
-    ring_last(*query_ring)
     for p in (1, 0):
         send_wait(p, 1)
         project(p, 1)
-    merge(1)
     for p in range(NP):
         for m in range(6):
+            spread(p, 0, m).wait_send()
             spread(p, 1 if p in LATE else 2, m).wait_send()
-        for step in (1, 2, 3):
-            first_copy(p, step).wait_send()
         for c in range(len(chunks(p))):
             for step in (1, 2, 3):
                 send(p, c, step).wait_send()
@@ -653,6 +623,8 @@
             for step in (2, 1, 3):
                 unsend(p, c, step).start()
 
+    fetch[4].wait()
+    weights[2].wait()
     expand_late(0)
     for p in EARLY:
         expand(p, 0)
@@ -660,6 +632,7 @@
     expand_late(1)
     for p in LATE:
         unsend_own(p)
+    ring_last(*query_ring)
     ring_end(*query_ring)
 
     def fact(r, j, i):
@@ -699,18 +672,17 @@
         restore(p, 0)
         back(p, 1, 0).start()
         back(p, 1, 3).start()
-    ring_forward(*result_ring)
     for p in EARLY:
         total, buffer, index = back_total(p, 2)
         buffer[index] = total
         for step in (2, 1, 3):
             unsend(p, 0, step).start()
         unsend_own(p)
+    ring_forward(*result_ring)
     for p in LATE:
         restore(p, 1)
         back(p, 1, 1).start()
         back(p, 1, 2).start()
-    ring_last(*result_ring)
     for p in LATE:
         back_join(p, 1)
     for p in EARLY:
@@ -720,6 +692,7 @@
         total, buffer, index = back_total(p, 1)
         buffer[index] = total
         last_start(p)
+    ring_last(*result_ring)
     ring_end(*result_ring)
     for j in range(2):
         s = moving[j]
@@ -797,7 +770,6 @@
         + each(lambda p, lanes: (4, 8, 16, lanes) if p in LATE else (4, 4, 2, 16, lanes))
         + each(lambda p, lanes: (4, groups(p), 16, lanes))
         + each(lambda p, lanes: (32 * groups(p), 16 * groups(p)))
-        + [pltpu.VMEM((256, 4 * UNITS), F32) for _ in range(NP - 1)]
         + each(lambda p, lanes: (2,) + ring_lead(p) + (16, widths(lanes)[0][1]))
         + each(lambda p, lanes: (3, 16, lanes))
         + each(lambda p, lanes: (2,) + ring_lead(p) + (16, lanes))

time: 87.5 us -> 87.2 us (level)
  no operation moved by 1% of the time
where the time goes in v3:
time: 87.2 us; the launch traced here: 86.8 us
  Pallas kernels  86 us (99%)
    pallas_call x1, Pallas kernels, shards(): pl.pallas_call(kernel, out_shape=shapes, in_specs=[smem, smem] + [anywher...  81.9 us
    pallas_call x1, Pallas kernels, shards(): pl.pallas_call(finish, out_shape=shapes, in_specs=[anywhere, anywhere, vm...  4.08 us

profile of v3, /device:TPU:0, one launch (start us, length us, event | category | flops | bytes accessed | tf_op | source)
XLA Modules:
  0.0 86.8 jit_solution(93526758565778567)
XLA Ops:
  0.6 81.9 %shard_map.148 = (bf16[8,128,512]{2,1,0:T(8,128)(2,1)}, bf16[8,128,512]{2,1,0:T(8,128)(2,1)}, bf16[8,7168]{1,0:T(8,128)(2,1)}) custom-call(s32[8]{0:T(128)} %lengths.1, s32[8]{0:T(128)} %dest.1, bf16[8,576,1024]{2,1,0:T(8,128)(2,1)} %bitcast.5, bf16[8,576,128]{2,1,0:T(8,128)(2,1)} %bitcast.6, bf16[8,576,128]{2,1,0:T(8,128)(2,1)} %bitcast.7, ...), custom_call_target="tpu_custom_call" | custom-call | tf_op jit(solution)/shard_map/pallas_call | solution.py:783
  82.6 4.1 %shard_map.149 = (bf16[8,128,512]{2,1,0:T(8,128)(2,1)}, bf16[8,128,512]{2,1,0:T(8,128)(2,1)}, bf16[8,7168]{1,0:T(8,128)(2,1)}) custom-call(bf16[8,128,512]{2,1,0:T(8,128)(2,1)} %get-tuple-element.6.first, bf16[8,128,512]{2,1,0:T(8,128)(2,1)} %get-tuple-element.7.second, bf16[8,7168]{1,0:T(8,128)(2,1)} %get-tuple-element.8.tokens), custom_call_target="tpu_custom_call" | custom-call | tf_op jit(solution)/shard_map/pallas_call | solution.py:823
